TPU v7x, 256 devices: a whole 4x4x8 slice. The times are simulated.
256 devices in a mesh: dp: 8 (over x, core), seq: 32 (over z, y).
Axes of the slice: x: 4, y: 4, z: 8, core: 2. Of those that a mesh axis runs over, the one named last changes fastest.
Arguments:
- query: bfloat16 [49152, 4096], P('seq', 'dp'), parts along dimension 1, may hold values from -6 to 6
- key_in: bfloat16 [49152, 4096], P('seq', 'dp'), parts along dimension 1, may hold values from -6 to 6
- value: bfloat16 [49152, 4096], P('seq', 'dp'), parts along dimension 1, may hold values from -6 to 6
- grad_out: bfloat16 [49152, 4096], P('seq', 'dp'), parts along dimension 1, may hold values from -6 to 6
Outputs:
- output: bfloat16 [49152, 4096], P('seq', 'dp'), parts along dimension 1
- grad_query: bfloat16 [49152, 4096], P('seq', 'dp'), parts along dimension 1
- grad_key: bfloat16 [49152, 4096], P('seq', 'dp'), parts along dimension 1
- grad_value: bfloat16 [49152, 4096], P('seq', 'dp'), parts along dimension 1
There are 8 independent parts, one for each index of `dp`. A program takes and returns all parts, laid end to end along the dimension named above; each array names one. Nothing has to cross between parts.
All inputs are finite; a program needn't handle non-finite values.
Results may differ from a plain program's by a relative error of at most 0.0021.
Values sent between devices are 32-bit elements; how exact they have to be, the bound alone decides.
No kernel may reach another device: no remote copies, remote signals or barrier semaphores. Data moves between devices by JAX's collectives and lax.ppermute only.
A program may use at most 192 MiB of HBM per device.

v0:
```python
import math

import jax
import jax.numpy as jnp
from jax import lax
from jax.sharding import PartitionSpec as P

DH = 128
SPAN = 512


def carried_in(value, axis, combine, identity, reverse):
    size, mine = (lax.axis_size(axis), lax.axis_index(axis))
    everything = lax.all_gather(value, axis)
    start = jnp.broadcast_to(jnp.asarray(identity, value.dtype), value.shape)

    def lap(k, before):
        at = size - 1 - k if reverse else k
        reached = at > mine if reverse else at < mine
        new = combine(before, everything[at])
        return jnp.where(reached, new, before)

    return lax.fori_loop(0, size, lap, start)


def on_device(query, key_in, value, grad_out):
    hp = lax.Precision.HIGHEST
    rows, width = query.shape
    heads = width // DH
    blocks = rows // SPAN
    scale = 1.0 / math.sqrt(DH * rows * lax.axis_size("seq"))

    def split(x):
        return x.reshape(blocks, SPAN, heads, DH)

    qb, kb, vb, gb = (split(query), split(key_in), split(value), split(grad_out))
    kv_blocks = jnp.einsum("nshk,nshv->nhkv", kb, vb, preferred_element_type=jnp.float32)
    qg_blocks = jnp.einsum("nthk,nthv->nhkv", qb, gb, preferred_element_type=jnp.float32)
    kv_own = jnp.sum(kv_blocks, axis=0)
    qg_own = jnp.sum(qg_blocks, axis=0)
    zeros = jnp.zeros((heads, DH, DH), jnp.float32)
    kv_prior = carried_in(kv_own, "seq", jnp.add, zeros, False)
    qg_later = carried_in(qg_own, "seq", jnp.add, zeros, True)
    causal = (jnp.arange(SPAN)[:, None] >= jnp.arange(SPAN)[None, :]).astype(jnp.float32)
    scores = (
        scale * causal * jnp.einsum("nthk,nshk->nhts", qb, kb, preferred_element_type=jnp.float32)
    ).astype(jnp.bfloat16)
    gscores = (
        scale * causal * jnp.einsum("nthv,nshv->nhts", gb, vb, preferred_element_type=jnp.float32)
    ).astype(jnp.bfloat16)
    local_out = jnp.einsum("nhts,nshv->nthv", scores, vb, preferred_element_type=jnp.float32)
    local_gq = jnp.einsum("nhts,nshk->nthk", gscores, kb, preferred_element_type=jnp.float32)
    local_gk = jnp.einsum("nhts,nthk->nshk", gscores, qb, preferred_element_type=jnp.float32)
    local_gv = jnp.einsum("nhts,nthv->nshv", scores, gb, preferred_element_type=jnp.float32)
    state_kv = kv_prior[None] + (jnp.cumsum(kv_blocks, axis=0) - kv_blocks)
    state_qg = qg_later[None] + (jnp.cumsum(qg_blocks[::-1], axis=0)[::-1] - qg_blocks)
    qf, kf, vf, gf = (
        qb.astype(jnp.float32),
        kb.astype(jnp.float32),
        vb.astype(jnp.float32),
        gb.astype(jnp.float32),
    )
    output = local_out + scale * jnp.einsum("nthk,nhkv->nthv", qf, state_kv, precision=hp)
    grad_query = local_gq + scale * jnp.einsum("nthv,nhkv->nthk", gf, state_kv, precision=hp)
    grad_key = local_gk + scale * jnp.einsum("nshv,nhkv->nshk", vf, state_qg, precision=hp)
    grad_value = local_gv + scale * jnp.einsum("nshk,nhkv->nshv", kf, state_qg, precision=hp)

    def back(x):
        return x.reshape(rows, width).astype(jnp.bfloat16)

    return (back(output), back(grad_query), back(grad_key), back(grad_value))


def solution(mesh):
    return jax.shard_map(
        on_device,
        mesh=mesh,
        in_specs=(P("seq", "dp"), P("seq", "dp"), P("seq", "dp"), P("seq", "dp")),
        out_specs=(P("seq", "dp"), P("seq", "dp"), P("seq", "dp"), P("seq", "dp")),
        check_vma=False,
    )
```

profile of v0, /device:TPU:38, one launch (start us, length us, event | category | flops | bytes accessed | tf_op | source)
XLA Modules:
  0.0 275.7 jit_solution(17763077413635992648)
XLA Ops:
  7.2 2.4 reshape.44
  9.6 2.8 %reshape.45 = bf16[3,512,4,128]{3,2,1,0:T(4,128)(2,1)S(1)} reshape(bf16[1536,512]{1,0:T(8,128)(2,1)} %param.10) | data formatting | bytes 3145728 | tf_op jit(solution)/shard_map/reshape | solution.py:34
  12.4 2.3 fusion.23
  14.8 2.5 reshape.46
  17.3 1.9 reshape.43
  19.1 2.6 copy.77
  21.8 2.2 fusion.24
  24.0 2.1 rev.6
  26.2 2.2 fusion.25
  28.4 1.9 multiply_convert_fusion.1
  30.4 1.9 multiply_convert_fusion
  32.3 3.7 %fusion.26 = f32[3,4,512,128]{3,2,1,0:T(8,128)} fusion(bf16[3,4,512,512]{3,2,1,0:T(8,128)(2,1)S(1)} %multiply_convert_fusion, bf16[3,512,4,128]{1,3,2,0:T(8,128)(2,1)S(1)} %copy.77), kind=kOutput, calls=%fused_computation.41 | convolution fusion | flops 805306368 | bytes 11010048 | tf_op jit(solution)/shard_map/nhts,nthk->nshk/dot_general | solution.py:53
  36.0 3.8 %fusion.6 = f32[3,4,512,128]{3,2,1,0:T(8,128)} fusion(bf16[3,4,512,512]{3,2,1,0:T(8,128)(2,1)S(1)} %multiply_convert_fusion.1, bf16[3,512,4,128]{3,2,1,0:T(4,128)(2,1)S(1)} %reshape.46), kind=kOutput, calls=%fused_computation.20 | convolution fusion | flops 805306368 | bytes 11010048 | tf_op jit(solution)/shard_map/nhts,nthv->nshv/dot_general | solution.py:54
  39.8 3.5 %fusion.16 = f32[3,4,512,128]{3,2,1,0:T(8,128)} fusion(bf16[3,4,512,512]{3,2,1,0:T(8,128)(2,1)S(1)} %multiply_convert_fusion.1, bf16[3,512,4,128]{3,2,1,0:T(4,128)(2,1)S(1)} %copy-done.1), kind=kOutput, calls=%fused_computation.30 | convolution fusion | flops 805306368 | bytes 11010048 | tf_op jit(solution)/shard_map/nhts,nshv->nthv/dot_general | solution.py:51
  43.3 3.5 %fusion.20 = f32[3,4,512,128]{3,2,1,0:T(8,128)} fusion(bf16[3,4,512,512]{3,2,1,0:T(8,128)(2,1)S(1)} %multiply_convert_fusion, bf16[3,512,4,128]{3,2,1,0:T(4,128)(2,1)S(1)} %copy-done.4), kind=kOutput, calls=%fused_computation.34 | convolution fusion | flops 805306368 | bytes 11010048 | tf_op jit(solution)/shard_map/nhts,nshk->nthk/dot_general | solution.py:52
  46.8 67.4 %all-gather.5.cloned.1.call-done = f32[128,128,128]{2,1,0:T(8,128)} async-done(((f32[4,128,128]{2,1,0:T(8,128)}), f32[128,128,128]{2,1,0:T(8,128)}) %all-gather.5.cloned.1.call-update) | async-done | bytes 8388624 | tf_op jit(solution)/shard_map/all_gather | solution.py:14
  114.2 56.3 %while.30 = (s32[]{:T(128)}, f32[4,128,128]{2,1,0:T(8,128)}, s32[]{:T(128)}, f32[32,4,128,128]{3,2,1,0:T(8,128)}, s32[]{:T(128)}, /*index=5*/s32[]{:T(128)}) while((s32[]{:T(128)}, f32[4,128,128]{2,1,0:T(8,128)}, s32[]{:T(128)}, f32[32,4,128,128]{3,2,1,0:T(8,128)}, s32[]{:T(128)}, /*index=5*/s32[]{:T(128)}) %tuple.86), condition=%wide.region_2.3_spmd.clone, body=%wide.region_1.0_spmd.clone.sunk | while | flops 196612 | bytes 786533 | solution.py:23
  115.9 1.8 add_select_fusion.4
  117.7 1.8 add_select_fusion.4
  119.4 1.8 add_select_fusion.4
  121.2 1.8 add_select_fusion.4
  122.9 1.8 add_select_fusion.4
  124.7 1.8 add_select_fusion.4
  126.5 1.8 add_select_fusion.4
  128.2 1.8 add_select_fusion.4
  130.0 1.8 add_select_fusion.4
  131.8 1.8 add_select_fusion.4
  133.5 1.8 add_select_fusion.4
  135.3 1.8 add_select_fusion.4
  137.1 1.8 add_select_fusion.4
  138.8 1.8 add_select_fusion.4
  140.6 1.8 add_select_fusion.4
  142.3 1.8 add_select_fusion.4
  144.1 1.8 add_select_fusion.4
  145.9 1.8 add_select_fusion.4
  149.4 1.8 add_select_fusion.4
  151.1 1.8 add_select_fusion.4
  152.9 1.8 add_select_fusion.4
  154.7 1.8 add_select_fusion.4
  156.4 1.8 add_select_fusion.4
  158.2 1.8 add_select_fusion.4
  167.0 1.8 add_select_fusion.4
  170.6 41.9 %all-gather.7.cloned.1.call-done = f32[128,128,128]{2,1,0:T(8,128)} async-done(((f32[4,128,128]{2,1,0:T(8,128)}), f32[128,128,128]{2,1,0:T(8,128)}) %all-gather.7.cloned.1.call-update) | async-done | bytes 8388624 | tf_op jit(solution)/shard_map/all_gather | solution.py:14
  212.5 34.2 %while.31 = (s32[]{:T(128)}, f32[4,128,128]{2,1,0:T(8,128)S(1)}, s32[]{:T(128)}, f32[32,4,128,128]{3,2,1,0:T(8,128)}, s32[]{:T(128)}, /*index=5*/s32[]{:T(128)}, s32[]{:T(128)}, s32[]{:T(128)}) while((s32[]{:T(128)}, f32[4,128,128]{2,1,0:T(8,128)S(1)}, s32[]{:T(128)}, f32[32,4,128,128]{3,2,1,0:T(8,128)}, s32[]{:T(128)}, ...), condition=%wide.region_6.7_spmd.clone, body=%wide.region_5.6_spmd.clone.sunk | while | flops 196616 | bytes 786595 | solution.py:23
  248.6 3.2 %fusion = bf16[3,512,4,128]{3,1,2,0:T(8,128)(2,1)S(1)} fusion(f32[3,4,512,128]{3,2,1,0:T(8,128)} %fusion.6, f32[3,4,128,128]{3,2,1,0:T(8,128)S(1)} %subtract_add_fusion, bf16[3,512,4,128]{3,2,1,0:T(4,128)(2,1)S(1)} %copy-done.5), kind=kOutput, calls=%fused_computation.5 | convolution fusion | flops 1210318848 | bytes 7077888 | tf_op jit(solution)/shard_map/nshk,nhkv->nshv/dot_general | solution.py:66
  253.7 2.0 fusion.3
  264.1 2.4 copy_bitcast_fusion.2
  266.6 2.3 copy_bitcast_fusion
  (78 shorter events, 57.9 us)
Async XLA Ops:
  7.2 107.1 %all-gather.5.cloned.1.call-start = ((), (), s32[]{:S(2)}) async-start(), calls=%async_computation | async-start | bytes 8650752 | tf_op jit(solution)/shard_map/all_gather | solution.py:14
  9.6 2.8 %copy-start.3 = (bf16[3,512,4,128]{3,2,1,0:T(4,128)(2,1)}, bf16[3,512,4,128]{3,2,1,0:T(4,128)(2,1)S(1)}, u32[]{:S(2)}) copy-start(bf16[3,512,4,128]{3,2,1,0:T(4,128)(2,1)S(1)} %reshape.44) | copy-start | bytes 4718596
  12.4 2.3 copy-start
  14.7 2.5 copy-start.11
  14.7 197.7 %all-gather.7.cloned.1.call-start = ((), (), s32[]{:S(2)}) async-start(), calls=%async_computation.1 | async-start | bytes 8650752 | tf_op jit(solution)/shard_map/all_gather | solution.py:14
  26.1 2.4 copy-start.4
  28.4 1.9 copy-start.1
  246.7 1.9 copy-start.5
  248.6 4.5 %copy-start.9 = (f32[4,128,128]{2,1,0:T(8,128)S(1)}, f32[4,128,128]{2,1,0:T(8,128)}, u32[]{:S(2)}) copy-start(f32[4,128,128]{2,1,0:T(8,128)} %get-tuple-element.193) | copy-start | bytes 786436
  248.6 4.5 %copy-start.10 = (f32[3,4,128,128]{3,2,1,0:T(8,128)S(1)}, f32[3,4,128,128]{3,2,1,0:T(8,128)}, u32[]{:S(2)}) copy-start(f32[3,4,128,128]{3,2,1,0:T(8,128)} %get-tuple-element.242) | copy-start | bytes 2359300
  251.8 1.9 copy-start.8
  255.7 1.9 copy-start.7
  257.6 1.7 copy-start.2
  257.6 2.4 copy-start.6
Sparse Core Ops, SparseCore 0:
  14.9 99.3 all-gather.4
  116.8 95.6 all-gather.6
where the time goes:
time: 280 us; the launch traced here: 276 us
  waiting for transfers between devices  109 us (39%)
  other arithmetic  93.7 us (33%)
  matrix products  31.4 us (11%)
  local copies, waits for them, and re-layouts  25.9 us (9%)
  between operations  14.3 us (5%)
    all_gather x2, waiting for transfers between devices, carried_in(): everything = lax.all_gather(value, axis)  109 us
    select_n x64, other arithmetic, lap(): return jnp.where(reached, new, before)  89.6 us
    reshape x5, local copies, waits for them, and re-layouts, split(): return x.reshape(blocks, SPAN, heads, DH)  12.1 us
    convert_element_type x6, local copies, waits for them, and re-layouts, back(): return x.reshape(rows, width).astype(jnp.bfloat16)  9.62 us
  transfers between devices with their start and end apart: 2, of which 2 were waited for; matrix products, arithmetic and copies ran while one was open for 32% of the time, Pallas kernels for 0%

commit v1 on v0

v1 whole, which is shorter than its diff:
```python
import functools
import math

import jax
import jax.numpy as jnp
from jax import lax
from jax.experimental import pallas as pl
from jax.experimental.pallas import tpu as pltpu
from jax.sharding import PartitionSpec as P

DH = 128
SPAN = 512
HALF = SPAN // 2
HEADS = 4
NY = 4
NZ = 8
LOCAL_FLOPS = 2_000_000_000
F32 = jnp.float32
BF16 = jnp.bfloat16
VM = pl.BlockSpec(memory_space=pltpu.VMEM)
SM = pl.BlockSpec(memory_space=pltpu.SMEM)
HB = pl.BlockSpec(memory_space=pltpu.HBM)


def dot(a, b, ca, cb):
    return lax.dot_general(a, b, (((ca,), (cb,)), ((), ())), preferred_element_type=F32)


def twice(x):
    return jnp.concatenate([x, x], axis=1)


def stacked(s, axis):
    hi = s.astype(BF16)
    lo = (s - hi.astype(F32)).astype(BF16)
    return jnp.concatenate([hi, lo], axis=axis)


def at(n, h):
    return slice(n * SPAN, (n + 1) * SPAN), slice(h * DH, (h + 1) * DH)


CHUNKS = ((0, 512), (512, 512), (1024, 256), (1280, 256))


def head_sums(me_ref, xs, d, out, cum):
    q, k, v, g = xs
    cols = pl.ds(pl.multiple_of(((me_ref[0] + d) & 3) * DH, DH), DH)
    state = {"kv": 0.0, "first": 0.0}

    def step(n):
        start, size = CHUNKS[n]
        block, r = start // SPAN, slice(start, start + size)
        qg = dot(q[r, cols], g[r, cols], 0, 0)
        state["kv"] = state["kv"] + dot(k[r, cols], v[r, cols], 0, 0)
        for j in range(min(block, cum.shape[0])):
            if block == j + 1 and start % SPAN == 0:
                cum[j, DH:] = qg
            else:
                cum[j, DH:] += qg
        if block == 0:
            state["first"] = state["first"] + qg
        if (start + size) % SPAN == 0 and block < cum.shape[0]:
            cum[block, :DH] = state["kv"]

    def finish():
        out[:DH] = state["kv"]
        out[DH:] = state["first"] + cum[0, DH:]

    return step, finish


def sums_kernel(me_ref, high_ref, up_ref, *refs):
    srcs, dsts, outs, cum, sems = refs[:4], refs[4:8], refs[8:11], refs[11], refs[12]
    copies = []
    for n, (start, size) in enumerate(CHUNKS):
        rows = pl.ds(start, size)
        copies.append([pltpu.make_async_copy(srcs[i].at[rows], dsts[i].at[rows], sems.at[n, i]) for i in range(4)])
    for row in copies:
        for c in row:
            c.start()
    heads = [head_sums(me_ref, dsts, d + 1, outs[d], cum.at[d]) for d in range(3)]
    for n in range(len(CHUNKS)):
        for c in copies[n]:
            c.wait()
        for step, _ in heads:
            step(n)
    for _, finish in heads:
        finish()


def device_sums(me, high, up, q, k, v, g):
    rows, width = q.shape
    one = jax.ShapeDtypeStruct((2 * DH, DH), F32)
    return pl.pallas_call(
        sums_kernel,
        in_specs=[SM] * 3 + [HB] * 4,
        out_specs=[VM] * 8,
        out_shape=[pltpu.VMEM((rows, width), BF16)] * 4 + [one] * 3 + [pltpu.VMEM((3, rows // SPAN - 1, 2 * DH, DH), F32)],
        scratch_shapes=[pltpu.SemaphoreType.DMA((len(CHUNKS), 4))],
        compiler_params=pltpu.CompilerParams(vmem_limit_bytes=16 * 2**20),
        name="device_sums",
    )(me, high, up, q, k, v, g)


def own_kernel(me_ref, q, k, v, g, out, cum):
    step, finish = head_sums(me_ref, (q, k, v, g), 0, out, cum.at[0])
    for n in range(len(CHUNKS)):
        step(n)
    finish()


def own_sums(me, xs):
    rows = xs[0].shape[0]
    return pl.pallas_call(
        own_kernel,
        in_specs=[SM] + [VM] * 4,
        out_specs=[VM] * 2,
        out_shape=[jax.ShapeDtypeStruct((2 * DH, DH), F32), pltpu.VMEM((1, rows // SPAN - 1, 2 * DH, DH), F32)],
        compiler_params=pltpu.CompilerParams(vmem_limit_bytes=8 * 2**20),
        cost_estimate=pl.CostEstimate(flops=100_000_000, bytes_accessed=1024, transcendentals=0),
        name="own_sums",
    )(me, *xs)


def local_kernel(scale, h, blocks, q_ref, k_ref, v_ref, g_ref, *refs):
    o_ref, gq_ref, gk_ref, gv_ref = refs[-4:]
    cols = slice(h * DH, (h + 1) * DH)
    t = lax.broadcasted_iota(jnp.int32, (HALF, HALF), 0)
    s = lax.broadcasted_iota(jnp.int32, (HALF, HALF), 1)
    keep = t >= s

    def lower(a, b):
        top = jnp.where(keep, scale * dot(a[:HALF], b[:HALF], 1, 1), 0.0).astype(BF16)
        low = scale * dot(a[HALF:], b, 1, 1)
        right = jnp.where(keep, low[:, HALF:], 0.0)
        return top, jnp.concatenate([low[:, :HALF].astype(BF16), right.astype(BF16)], axis=1)

    def across(top, low, x):
        return jnp.concatenate([dot(top, x[:HALF], 1, 0), dot(low, x, 1, 0)], axis=0)

    def down(top, low, x):
        both = dot(low, x[HALF:], 0, 0)
        return jnp.concatenate([dot(top, x[:HALF], 0, 0) + both[:HALF], both[HALF:]], axis=0)

    for n in range(blocks):
        r = slice(n * SPAN, (n + 1) * SPAN)
        q, k, v, g = q_ref[r, cols], k_ref[r, cols], v_ref[r, cols], g_ref[r, cols]
        s0, s1 = lower(q, k)
        d0, d1 = lower(g, v)
        o_ref[r, cols] = across(s0, s1, v)
        gq_ref[r, cols] = across(d0, d1, k)
        gk_ref[r, cols] = down(d0, d1, q)
        gv_ref[r, cols] = down(s0, s1, g)


def local_products(scale, h, xs, parts):
    rows, width = xs[0].shape
    blocks = rows // SPAN
    return pl.pallas_call(
        functools.partial(local_kernel, scale, h, blocks),
        in_specs=[VM] * (4 + len(parts)),
        out_specs=[VM] * 4,
        out_shape=[pltpu.VMEM((rows, width), F32)] * 4,
        input_output_aliases={4 + i: i for i in range(len(parts))},
        compiler_params=pltpu.CompilerParams(vmem_limit_bytes=16 * 2**20),
        cost_estimate=pl.CostEstimate(flops=LOCAL_FLOPS, bytes_accessed=1024, transcendentals=0),
        name="local_products",
    )(*xs, *parts)


def ready_kernel(me_ref, g0, g1, g2, g3, pair, *outs):
    y, z = me_ref[0] & 3, me_ref[0] >> 2
    got = [(r[:DH], r[DH:]) for r in (g0, g1, g2, g3)]

    def when(c, x):
        return jnp.where(c, x, 0.0)

    kv = when((z & 1) != 0, pair[:DH])
    qg = when((z & 1) == 0, pair[DH:])
    for e, out in enumerate(outs):
        dst = (y + e) & 3
        a, b = kv, qg
        for d in range(NY):
            src = (y - d) & 3
            a = a + when(src < dst, got[d][0])
            b = b + when(src > dst, got[d][1])
        out[:DH] = a
        out[DH:] = b


def make_ready(me, *arrays):
    return pl.pallas_call(
        ready_kernel,
        in_specs=[SM] + [VM] * len(arrays),
        out_specs=[VM] * NY,
        out_shape=[jax.ShapeDtypeStruct((2 * DH, DH), F32)] * NY,
        compiler_params=pltpu.CompilerParams(vmem_limit_bytes=8 * 2**20),
        name="make_ready",
    )(me, *arrays)


def carry_kernel(scale, steps, blocks, me_ref, *refs):
    xs, parts, cums, refs = refs[:4], refs[4:8], refs[8:10], refs[10:]
    priors, outs, stage, sems = refs[: len(steps)], refs[-6:-2], refs[-2], refs[-1]
    q, k, v, g = xs
    copies = []
    for i, (d, prior) in enumerate(zip(steps, priors)):
        h = (me_ref[0] - d) & 3
        cols = pl.ds(pl.multiple_of(h * DH, DH), DH)
        cum = cums[1].at[HEADS - 1 - d] if d else cums[0].at[0]
        for n in range(blocks):
            kv, qg = prior[:DH], prior[DH:]
            if n > 0:
                kv = kv + cum[n - 1, :DH]
            if n < blocks - 1:
                qg = qg + cum[n, DH:]
            kv, qg = kv * scale, qg * scale
            r = pl.ds(n * SPAN, SPAN)
            todo = ((q, stacked(kv, 0), 0), (g, stacked(kv, 1), 1), (v, stacked(qg, 1), 1), (k, stacked(qg, 0), 0))
            for j, (x, w, c) in enumerate(todo):
                add = dot(twice(x[r, cols]), w, 1, c)
                stage[i, j, r] = (parts[j][r, cols] + add).astype(BF16)
                copy = pltpu.make_async_copy(stage.at[i, j, r], outs[j].at[r, cols], sems.at[i, j, n])
                copy.start()
                copies.append(copy)
    for copy in copies:
        copy.wait()


def add_carry(scale, me, steps, xs, parts, cums, priors, before):
    rows, width = xs[0].shape
    blocks = rows // SPAN
    m = len(steps)
    return pl.pallas_call(
        functools.partial(carry_kernel, scale, steps, blocks),
        in_specs=[SM] + [VM] * (10 + m) + [HB] * len(before),
        out_specs=[HB] * 4,
        out_shape=[pltpu.HBM((rows, width), BF16)] * 4,
        input_output_aliases={11 + m + i: i for i in range(len(before))},
        scratch_shapes=[pltpu.VMEM((m, 4, rows, DH), BF16), pltpu.SemaphoreType.DMA((m, 4, blocks))],
        compiler_params=pltpu.CompilerParams(vmem_limit_bytes=16 * 2**20),
        cost_estimate=pl.CostEstimate(flops=m * 1_500_000_000, bytes_accessed=1024, transcendentals=0),
        name="add_carry",
    )(me, *xs, *parts, *cums, *priors, *before)


def moves(zmap, ymap):
    return [(z * NY + y, zmap(z) * NY + ymap(y)) for z in range(NZ) for y in range(NY)]


def on_device(query, key_in, value, grad_out):
    rows = query.shape[0]
    scale = 1.0 / math.sqrt(DH * rows * lax.axis_size("seq"))
    blocks = rows // SPAN
    index = lax.axis_index("seq")
    me = index.reshape(1)
    inputs = [pltpu.with_memory_space_constraint(x, pltpu.HBM) for x in (query, key_in, value, grad_out)]

    def swap(x, zmap):
        return lax.ppermute(x, "seq", moves(zmap, lambda b: b))

    def turn(x, d):
        return lax.ppermute(x, "seq", moves(lambda a: a, lambda b: (b + d) % NY))

    high, up = index >= NY * NZ // 2, (index & (2 * NY)) != 0
    flags = [c.astype(jnp.int32).reshape(1) for c in (high, up)]
    q, k, v, g, *own, others = device_sums(me, *flags, *inputs)
    xs = (q, k, v, g)
    sent = [turn(own[d - 1], d) for d in range(1, NY)]
    mine, inner = own_sums(me, xs)
    got = [mine] + sent
    parts = ()
    for h in range(HEADS):
        parts = local_products(scale, h, xs, parts)
    total = got[0] + got[1] + got[2] + got[3]
    pair = swap(total, lambda a: a ^ 1)
    total = total + pair
    four = swap(jnp.where(up, total[DH:], total[:DH]), lambda a: a ^ 3)
    across = jnp.where(high, total[DH:], total[:DH])
    eight = swap(across, lambda a: a ^ 5), swap(across, lambda a: 7 - a)
    eight = eight[0] + eight[1]
    last = jnp.concatenate(
        [
            jnp.where(up, four, 0.0) + jnp.where(high, eight, 0.0),
            jnp.where(up, 0.0, four) + jnp.where(high, 0.0, eight),
        ],
        axis=0,
    )
    ready = [x + last for x in make_ready(me, *got, pair)]
    prior = {0: ready[0]} | {d: turn(ready[d], d) for d in (2, 3, 1)}
    outs = ()
    for steps in ((0,), (3,), (2, 1)):
        outs = add_carry(scale, me, steps, xs, parts, (inner, others), [prior[d] for d in steps], outs)
    return tuple(outs)


def solution(mesh):
    spec = P("seq", "dp")
    return jax.shard_map(
        on_device,
        mesh=mesh,
        in_specs=(spec,) * 4,
        out_specs=(spec,) * 4,
        check_vma=False,
    )
```

time: 280 us -> 47 us (0.17); the launches traced: 276 us -> 46.2 us
  waiting for transfers between devices: 109 us -> 7.56 us
  other arithmetic: 93.7 us -> 0.12 us
  matrix products: 31.4 us -> 0 us
  local copies, waits for them, and re-layouts: 25.9 us -> 0 us
  starting transfers between devices: 0.08 us -> 19 us
  Pallas kernels: 0 us -> 18.6 us
  between operations: 14.3 us -> 0.92 us
    all_gather x2 -> x0, waiting for transfers between devices: 109 us -> none  [carried_in(): everything = lax.all_gather(value, axis)]
    select_n x64 -> x1, other arithmetic: 89.6 us -> 0.01 us  [on_device(): across = jnp.where(high, total[DH:], total[:DH])]
    dot_general x12 -> x0, matrix products: 31.4 us -> none  [the longest x1 3.76 us: on_device(): jnp.einsum('nhts,nthv->nshv', scores, gb, preferred_element_type=jnp.floa...]
    ppermute x0 -> x10, starting transfers between devices: none -> 19 us  [the longest x6 11.8 us: turn(): return lax.ppermute(x, 'seq', moves(lambda a: a, lambda b: (b + d) % NY))]
    pallas_call x0 -> x10, Pallas kernels: none -> 18.6 us  [the longest x4 8.2 us: local_products(): pl.pallas_call(functools.partial(local_kernel, scale, h, blocks), in_spec...]
    reshape x5 -> x0, local copies, waits for them, and re-layouts: 12.1 us -> none  [split(): return x.reshape(blocks, SPAN, heads, DH)]
    convert_element_type x6 -> x0, local copies, waits for them, and re-layouts: 9.62 us -> none  [back(): return x.reshape(rows, width).astype(jnp.bfloat16)]
    ppermute x0 -> x10, waiting for transfers between devices: none -> 7.56 us  [the longest x4 6.73 us: swap(): return lax.ppermute(x, 'seq', moves(zmap, lambda b: b))]
  transfers between devices with their start and end apart: 2 -> 10, of which waited for: 2 -> 5; matrix products, arithmetic and copies ran while one was open for 32% -> 0% of each run, Pallas kernels for 0% -> 27%
where the time goes in v1:
time: 47 us; the launch traced here: 46.2 us
  starting transfers between devices  19 us (40%)
  Pallas kernels  18.6 us (40%)
  waiting for transfers between devices  7.56 us (16%)
  between operations  0.92 us (2%)
    ppermute x6, starting transfers between devices, turn(): return lax.ppermute(x, 'seq', moves(lambda a: a, lambda b: (b + d) % NY))  11.8 us
    pallas_call x4, Pallas kernels, local_products(): pl.pallas_call(functools.partial(local_kernel, scale, h, blocks), in_spec...  8.2 us
    ppermute x4, starting transfers between devices, swap(): return lax.ppermute(x, 'seq', moves(zmap, lambda b: b))  7.24 us
    ppermute x4, waiting for transfers between devices, swap(): return lax.ppermute(x, 'seq', moves(zmap, lambda b: b))  6.73 us
    pallas_call x3, Pallas kernels, add_carry(): pl.pallas_call(functools.partial(carry_kernel, scale, steps, blocks), in_...  6.36 us
    pallas_call x1, Pallas kernels, device_sums(): pl.pallas_call(sums_kernel, in_specs=[SM] * 3 + [HB] * 4, out_specs=[VM]...  3.45 us
  transfers between devices with their start and end apart: 10, of which 5 were waited for; matrix products, arithmetic and copies ran while one was open for 0% of the time, Pallas kernels for 27%

profile of v1, /device:TPU:38, one launch (start us, length us, event | category | flops | bytes accessed | tf_op | source)
XLA Modules:
  0.0 46.2 jit_solution(527447442505083391)
XLA Ops:
  0.6 3.5 %device_sums.1 = (bf16[1536,512]{1,0:T(8,128)(2,1)S(1)}, bf16[1536,512]{1,0:T(8,128)(2,1)S(1)}, bf16[1536,512]{1,0:T(8,128)(2,1)S(1)}, bf16[1536,512]{1,0:T(8,12...) custom-call(s32[1]{0:T(128)} %bitcast.me_ref, ...), custom_call_target="tpu_custom_call" | custom-call | tf_op jit(solution)/shard_map/device_sums/pallas_call | solution.py:95
  4.1 1.7 %collective-permute-start = (f32[256,128]{1,0:T(8,128)S(1)}, f32[256,128]{1,0:T(8,128)S(1)}, u32[]{:S(2)}, u32[]{:S(2)}) collective-permute-start(f32[256,128]{1,0:T(8,128)S(1)} %get-tuple-element.65), channel_id=1, source_target_pairs={{0,1},{1,2},{2,3},{3,0},{4,5},{5,6},{6,7},{7,4},{8,9},{9,10},{10,1... | collective-permute-start | bytes 393224 | tf_op jit(solution)/shard_map/ppermute | solution.py:264
  5.8 2.9 %collective-permute-start.1 = (f32[256,128]{1,0:T(8,128)S(1)}, f32[256,128]{1,0:T(8,128)S(1)}, u32[]{:S(2)}, u32[]{:S(2)}) collective-permute-start(f32[256,128]{1,0:T(8,128)S(1)} %get-tuple-element.66), channel_id=1, source_target_pairs={{0,2},{1,3},{2,0},{3,1},{4,6},{5,7},{6,4},{7,5},{8,10},{9,11},{10,... | collective-permute-start | bytes 393224 | tf_op jit(solution)/shard_map/ppermute | solution.py:264
  8.7 1.3 %collective-permute-start.2 = (f32[256,128]{1,0:T(8,128)S(1)}, f32[256,128]{1,0:T(8,128)S(1)}, u32[]{:S(2)}, u32[]{:S(2)}) collective-permute-start(f32[256,128]{1,0:T(8,128)S(1)} %get-tuple-element.67), channel_id=1, source_target_pairs={{0,3},{1,0},{2,1},{3,2},{4,7},{5,4},{6,5},{7,6},{8,11},{9,8},{10,9... | collective-permute-start | bytes 393224 | tf_op jit(solution)/shard_map/ppermute | solution.py:264
  10.0 2.1 %local_products.4 = (f32[1536,512]{1,0:T(8,128)S(1)}, f32[1536,512]{1,0:T(8,128)S(1)}, f32[1536,512]{1,0:T(8,128)S(1)}, f32[1536,512]{1,0:T(8,128)S(1)}) custom-call(bf16[1536,512]{1,0:T(8,128)(2,1)S(1)} %get-tuple-element.42.q_ref.q.refs_0_, bf16[1536,512]{1,0:T(8,128)(2,1)S(1)} %get-tuple-element.43.k_ref.k.refs_1_, ...), custom_call_target="tpu_custom_call" | custom-call | flops 2000000000 | bytes 1024 | tf_op jit(solution)/shard_map/local_products/pallas_call | solution.py:160
  12.1 0.4 own_sums.1
  12.5 2.1 %local_products.5 = (f32[1536,512]{1,0:T(8,128)S(1)}, f32[1536,512]{1,0:T(8,128)S(1)}, f32[1536,512]{1,0:T(8,128)S(1)}, f32[1536,512]{1,0:T(8,128)S(1)}) custom-call(bf16[1536,512]{1,0:T(8,128)(2,1)S(1)} %get-tuple-element.42.q_ref.q.refs_0_, ...), custom_call_target="tpu_custom_call", output_to_operand_aliasing={{0}: (4, {}), {1}: (5, {}), {2}: (6, {}), {3}: (7, {})} | custom-call | flops 2000000000 | bytes 1024 | tf_op jit(solution)/shard_map/local_products/pallas_call | solution.py:160
  14.5 0.0 collective-permute-done.g1
  14.6 0.1 collective-permute-done.1.g2
  14.7 0.0 collective-permute-done.2.g3
  14.7 0.2 collective-permute-start.3
  14.9 2.0 %local_products.6 = (f32[1536,512]{1,0:T(8,128)S(1)}, f32[1536,512]{1,0:T(8,128)S(1)}, f32[1536,512]{1,0:T(8,128)S(1)}, f32[1536,512]{1,0:T(8,128)S(1)}) custom-call(bf16[1536,512]{1,0:T(8,128)(2,1)S(1)} %get-tuple-element.42.q_ref.q.refs_0_, ...), custom_call_target="tpu_custom_call", output_to_operand_aliasing={{0}: (4, {}), {1}: (5, {}), {2}: (6, {}), {3}: (7, {})} | custom-call | flops 2000000000 | bytes 1024 | tf_op jit(solution)/shard_map/local_products/pallas_call | solution.py:160
  17.0 2.8 %collective-permute-done.3.pair = f32[256,128]{1,0:T(8,128)S(1)} collective-permute-done((f32[256,128]{1,0:T(8,128)S(1)}, f32[256,128]{1,0:T(8,128)S(1)}, u32[]{:S(2)}, u32[]{:S(2)}) %collective-permute-start.3) | collective-permute-done | bytes 131104 | tf_op jit(solution)/shard_map/ppermute | solution.py:261
  19.8 5.9 %collective-permute-start.5 = (f32[128,128]{1,0:T(8,128)S(1)}, f32[128,128]{1,0:T(8,128)S(1)}, u32[]{:S(2)}, u32[]{:S(2)}) collective-permute-start(f32[128,128]{1,0:T(8,128)S(1)} %get-tuple-element.86), channel_id=1, source_target_pairs={{0,20},{1,21},{2,22},{3,23},{4,16},{5,17},{6,18},{7,19},{8,28},{9,... | collective-permute-start | bytes 196616 | tf_op jit(solution)/shard_map/ppermute | solution.py:261
  25.7 1.0 %collective-permute-start.6 = (f32[128,128]{1,0:T(8,128)S(1)}, f32[128,128]{1,0:T(8,128)S(1)}, u32[]{:S(2)}, u32[]{:S(2)}) collective-permute-start(f32[128,128]{1,0:T(8,128)S(1)} %get-tuple-element.86), channel_id=1, source_target_pairs={{0,28},{1,29},{2,30},{3,31},{4,24},{5,25},{6,26},{7,27},{8,20},{9,... | collective-permute-start | bytes 196616 | tf_op jit(solution)/shard_map/ppermute | solution.py:261
  26.7 0.1 collective-permute-start.4
  26.8 2.0 %local_products.7 = (f32[1536,512]{1,0:T(8,128)S(1)}, f32[1536,512]{1,0:T(8,128)S(1)}, f32[1536,512]{1,0:T(8,128)S(1)}, f32[1536,512]{1,0:T(8,128)S(1)}) custom-call(bf16[1536,512]{1,0:T(8,128)(2,1)S(1)} %get-tuple-element.42.q_ref.q.refs_0_, ...), custom_call_target="tpu_custom_call", output_to_operand_aliasing={{0}: (4, {}), {1}: (5, {}), {2}: (6, {}), {3}: (7, {})} | custom-call | flops 2000000000 | bytes 1024 | tf_op jit(solution)/shard_map/local_products/pallas_call | solution.py:160
  28.9 0.2 make_ready.1
  29.1 2.6 %collective-permute-done.4 = f32[128,128]{1,0:T(8,128)S(1)} collective-permute-done((f32[128,128]{1,0:T(8,128)S(1)}, f32[128,128]{1,0:T(8,128)S(1)}, u32[]{:S(2)}, u32[]{:S(2)}) %collective-permute-start.4) | collective-permute-done | bytes 65568 | tf_op jit(solution)/shard_map/ppermute | solution.py:261
  31.7 0.0 collective-permute-done.5
  31.7 1.3 %collective-permute-done.6 = f32[128,128]{1,0:T(8,128)S(1)} collective-permute-done((f32[128,128]{1,0:T(8,128)S(1)}, f32[128,128]{1,0:T(8,128)S(1)}, u32[]{:S(2)}, u32[]{:S(2)}) %collective-permute-start.6) | collective-permute-done | bytes 65568 | tf_op jit(solution)/shard_map/ppermute | solution.py:261
  33.1 2.7 %collective-permute-start.7 = (f32[256,128]{1,0:T(8,128)S(1)}, f32[256,128]{1,0:T(8,128)S(1)}, u32[]{:S(2)}, u32[]{:S(2)}) collective-permute-start(f32[256,128]{1,0:T(8,128)S(1)} %get-tuple-element.85), channel_id=1, source_target_pairs={{0,2},{1,3},{2,0},{3,1},{4,6},{5,7},{6,4},{7,5},{8,10},{9,11},{10,... | collective-permute-start | bytes 393224 | tf_op jit(solution)/shard_map/ppermute | solution.py:264
  35.7 0.4 collective-permute-start.8
  36.2 2.8 %collective-permute-start.9 = (f32[256,128]{1,0:T(8,128)S(1)}, f32[256,128]{1,0:T(8,128)S(1)}, u32[]{:S(2)}, u32[]{:S(2)}) collective-permute-start(f32[256,128]{1,0:T(8,128)S(1)} %get-tuple-element.84), channel_id=1, source_target_pairs={{0,3},{1,0},{2,1},{3,2},{4,7},{5,4},{6,5},{7,6},{8,11},{9,8},{10,9... | collective-permute-start | bytes 393224 | tf_op jit(solution)/shard_map/ppermute | solution.py:264
  39.0 1.8 %add_carry.3 = (bf16[1536,512]{1,0:T(8,128)(2,1)}, bf16[1536,512]{1,0:T(8,128)(2,1)}, bf16[1536,512]{1,0:T(8,128)(2,1)}, bf16[1536,512]{1,0:T(8,128)(2,1)}) custom-call(s32[1]{0:T(128)} %bitcast.me_ref, bf16[1536,512]{1,0:T(8,128)(2,1)S(1)} %get-tuple-element.42.q_ref.q.refs_0_, bf16[1536,512]{1,0:T(8,128)(2,1)S(1)} %get-tuple-element.43.k_ref.k.refs_1_, ...), custom_call_target="tpu_custom_call" | custom-call | flops 1500000000 | bytes 1024 | tf_op jit(solution)/shard_map/add_carry/pallas_call | solution.py:235
  40.8 0.7 %collective-permute-done.9.refs_10_ = f32[256,128]{1,0:T(8,128)S(1)} collective-permute-done((f32[256,128]{1,0:T(8,128)S(1)}, f32[256,128]{1,0:T(8,128)S(1)}, u32[]{:S(2)}, u32[]{:S(2)}) %collective-permute-start.9) | collective-permute-done | bytes 131104 | tf_op jit(solution)/shard_map/ppermute | solution.py:264
  41.5 1.8 %add_carry.4 = (bf16[1536,512]{1,0:T(8,128)(2,1)}, bf16[1536,512]{1,0:T(8,128)(2,1)}, bf16[1536,512]{1,0:T(8,128)(2,1)}, bf16[1536,512]{1,0:T(8,128)(2,1)}) custom-call(s32[1]{0:T(128)} %bitcast.me_ref, bf16[1536,512]{1,0:T(8,128)(2,1)S(1)} %get-tuple-element.42.q_ref.q.refs_0_, ...), custom_call_target="tpu_custom_call", output_to_operand_aliasing={{0}: (12, {}), {1}: (13, {}), {2}: (14, {}), {3}: (15, {})} | custom-call | flops 1500000000 | bytes 1024 | tf_op jit(solution)/shard_map/add_carry/pallas_call | solution.py:235
  43.3 0.0 collective-permute-done.7.refs_10_
  43.3 0.0 collective-permute-done.8.refs_11_
  43.3 2.8 %add_carry.5 = (bf16[1536,512]{1,0:T(8,128)(2,1)}, bf16[1536,512]{1,0:T(8,128)(2,1)}, bf16[1536,512]{1,0:T(8,128)(2,1)}, bf16[1536,512]{1,0:T(8,128)(2,1)}) custom-call(s32[1]{0:T(128)} %bitcast.me_ref, bf16[1536,512]{1,0:T(8,128)(2,1)S(1)} %get-tuple-element.42.q_ref.q.refs_0_, ...), custom_call_target="tpu_custom_call", output_to_operand_aliasing={{0}: (13, {}), {1}: (14, {}), {2}: (15, {}), {3}: (16, {})} | custom-call | flops 3000000000 | bytes 1024 | tf_op jit(solution)/shard_map/add_carry/pallas_call | solution.py:235
  (5 shorter events, 0.1 us)
Async XLA Ops:
  4.1 10.5 %collective-permute-start = (f32[256,128]{1,0:T(8,128)S(1)}, f32[256,128]{1,0:T(8,128)S(1)}, u32[]{:S(2)}, u32[]{:S(2)}) collective-permute-start(f32[256,128]{1,0:T(8,128)S(1)} %get-tuple-element.65), channel_id=1, source_target_pairs={{0,1},{1,2},{2,3},{3,0},{4,5},{5,6},{6,7},{7,4},{8,9},{9,10},{10,1... | collective-permute-start | bytes 393224 | tf_op jit(solution)/shard_map/ppermute | solution.py:264
  5.8 8.9 %collective-permute-start.1 = (f32[256,128]{1,0:T(8,128)S(1)}, f32[256,128]{1,0:T(8,128)S(1)}, u32[]{:S(2)}, u32[]{:S(2)}) collective-permute-start(f32[256,128]{1,0:T(8,128)S(1)} %get-tuple-element.66), channel_id=1, source_target_pairs={{0,2},{1,3},{2,0},{3,1},{4,6},{5,7},{6,4},{7,5},{8,10},{9,11},{10,... | collective-permute-start | bytes 393224 | tf_op jit(solution)/shard_map/ppermute | solution.py:264
  8.7 6.0 %collective-permute-start.2 = (f32[256,128]{1,0:T(8,128)S(1)}, f32[256,128]{1,0:T(8,128)S(1)}, u32[]{:S(2)}, u32[]{:S(2)}) collective-permute-start(f32[256,128]{1,0:T(8,128)S(1)} %get-tuple-element.67), channel_id=1, source_target_pairs={{0,3},{1,0},{2,1},{3,2},{4,7},{5,4},{6,5},{7,6},{8,11},{9,8},{10,9... | collective-permute-start | bytes 393224 | tf_op jit(solution)/shard_map/ppermute | solution.py:264
  14.7 5.1 %collective-permute-start.3 = (f32[256,128]{1,0:T(8,128)S(1)}, f32[256,128]{1,0:T(8,128)S(1)}, u32[]{:S(2)}, u32[]{:S(2)}) collective-permute-start(f32[256,128]{1,0:T(8,128)S(1)} %add_add_fusion), channel_id=1, source_target_pairs={{0,4},{1,5},{2,6},{3,7},{4,0},{5,1},{6,2},{7,3},{8,12},{9,13},{10,... | collective-permute-start | bytes 393224 | tf_op jit(solution)/shard_map/ppermute | solution.py:261
  19.8 11.9 %collective-permute-start.5 = (f32[128,128]{1,0:T(8,128)S(1)}, f32[128,128]{1,0:T(8,128)S(1)}, u32[]{:S(2)}, u32[]{:S(2)}) collective-permute-start(f32[128,128]{1,0:T(8,128)S(1)} %get-tuple-element.86), channel_id=1, source_target_pairs={{0,20},{1,21},{2,22},{3,23},{4,16},{5,17},{6,18},{7,19},{8,28},{9,... | collective-permute-start | bytes 196616 | tf_op jit(solution)/shard_map/ppermute | solution.py:261
  25.7 7.3 %collective-permute-start.6 = (f32[128,128]{1,0:T(8,128)S(1)}, f32[128,128]{1,0:T(8,128)S(1)}, u32[]{:S(2)}, u32[]{:S(2)}) collective-permute-start(f32[128,128]{1,0:T(8,128)S(1)} %get-tuple-element.86), channel_id=1, source_target_pairs={{0,28},{1,29},{2,30},{3,31},{4,24},{5,25},{6,26},{7,27},{8,20},{9,... | collective-permute-start | bytes 196616 | tf_op jit(solution)/shard_map/ppermute | solution.py:261
  26.7 5.0 %collective-permute-start.4 = (f32[128,128]{1,0:T(8,128)S(1)}, f32[128,128]{1,0:T(8,128)S(1)}, u32[]{:S(2)}, u32[]{:S(2)}) collective-permute-start(f32[128,128]{1,0:T(8,128)S(1)} %get-tuple-element.87), channel_id=1, source_target_pairs={{0,12},{1,13},{2,14},{3,15},{4,8},{5,9},{6,10},{7,11},{8,4},{9,5},... | collective-permute-start | bytes 196616 | tf_op jit(solution)/shard_map/ppermute | solution.py:261
  33.1 10.2 %collective-permute-start.7 = (f32[256,128]{1,0:T(8,128)S(1)}, f32[256,128]{1,0:T(8,128)S(1)}, u32[]{:S(2)}, u32[]{:S(2)}) collective-permute-start(f32[256,128]{1,0:T(8,128)S(1)} %get-tuple-element.85), channel_id=1, source_target_pairs={{0,2},{1,3},{2,0},{3,1},{4,6},{5,7},{6,4},{7,5},{8,10},{9,11},{10,... | collective-permute-start | bytes 393224 | tf_op jit(solution)/shard_map/ppermute | solution.py:264
  35.7 7.6 %collective-permute-start.8 = (f32[256,128]{1,0:T(8,128)S(1)}, f32[256,128]{1,0:T(8,128)S(1)}, u32[]{:S(2)}, u32[]{:S(2)}) collective-permute-start(f32[256,128]{1,0:T(8,128)S(1)} %get-tuple-element.83), channel_id=1, source_target_pairs={{0,1},{1,2},{2,3},{3,0},{4,5},{5,6},{6,7},{7,4},{8,9},{9,10},{10,1... | collective-permute-start | bytes 393224 | tf_op jit(solution)/shard_map/ppermute | solution.py:264
  36.2 5.3 %collective-permute-start.9 = (f32[256,128]{1,0:T(8,128)S(1)}, f32[256,128]{1,0:T(8,128)S(1)}, u32[]{:S(2)}, u32[]{:S(2)}) collective-permute-start(f32[256,128]{1,0:T(8,128)S(1)} %get-tuple-element.84), channel_id=1, source_target_pairs={{0,3},{1,0},{2,1},{3,2},{4,7},{5,4},{6,5},{7,6},{8,11},{9,8},{10,9... | collective-permute-start | bytes 393224 | tf_op jit(solution)/shard_map/ppermute | solution.py:264

commit v2 on v1

--- a/solution.py
+++ b/solution.py
@@ -216,14 +216,16 @@
             if n < blocks - 1:
                 qg = qg + cum[n, DH:]
             kv, qg = kv * scale, qg * scale
-            r = pl.ds(n * SPAN, SPAN)
             todo = ((q, stacked(kv, 0), 0), (g, stacked(kv, 1), 1), (v, stacked(qg, 1), 1), (k, stacked(qg, 0), 0))
-            for j, (x, w, c) in enumerate(todo):
-                add = dot(twice(x[r, cols]), w, 1, c)
-                stage[i, j, r] = (parts[j][r, cols] + add).astype(BF16)
-                copy = pltpu.make_async_copy(stage.at[i, j, r], outs[j].at[r, cols], sems.at[i, j, n])
-                copy.start()
-                copies.append(copy)
+            end = n == blocks - 1 and i == len(steps) - 1
+            for m, part in enumerate((HALF, HALF) if end else (SPAN,)):
+                r = pl.ds(n * SPAN + m * HALF, part)
+                for j, (x, w, c) in enumerate(todo):
+                    add = dot(twice(x[r, cols]), w, 1, c)
+                    stage[i, j, r] = (parts[j][r, cols] + add).astype(BF16)
+                    copy = pltpu.make_async_copy(stage.at[i, j, r], outs[j].at[r, cols], sems.at[i, j, n + m])
+                    copy.start()
+                    copies.append(copy)
     for copy in copies:
         copy.wait()
 
@@ -238,7 +240,7 @@
         out_specs=[HB] * 4,
         out_shape=[pltpu.HBM((rows, width), BF16)] * 4,
         input_output_aliases={11 + m + i: i for i in range(len(before))},
-        scratch_shapes=[pltpu.VMEM((m, 4, rows, DH), BF16), pltpu.SemaphoreType.DMA((m, 4, blocks))],
+        scratch_shapes=[pltpu.VMEM((m, 4, rows, DH), BF16), pltpu.SemaphoreType.DMA((m, 4, blocks + 1))],
         compiler_params=pltpu.CompilerParams(vmem_limit_bytes=16 * 2**20),
         cost_estimate=pl.CostEstimate(flops=m * 1_500_000_000, bytes_accessed=1024, transcendentals=0),
         name="add_carry",
@@ -290,7 +292,7 @@
     ready = [x + last for x in make_ready(me, *got, pair)]
     prior = {0: ready[0]} | {d: turn(ready[d], d) for d in (2, 3, 1)}
     outs = ()
-    for steps in ((0,), (3,), (2, 1)):
+    for steps in ((0,), (1, 2, 3)):
         outs = add_carry(scale, me, steps, xs, parts, (inner, others), [prior[d] for d in steps], outs)
     return tuple(outs)
 

time: 47 us -> 46 us (0.979)
  waiting for transfers between devices: 7.56 us -> 8.43 us
  Pallas kernels: 18.6 us -> 17.8 us
  starting transfers between devices: 19 us -> 18.4 us
    ppermute x6, waiting for transfers between devices: 0.83 us -> 1.7 us  [turn(): return lax.ppermute(x, 'seq', moves(lambda a: a, lambda b: (b + d) % NY))]
    pallas_call x3 -> x2, Pallas kernels: 6.36 us -> 5.54 us  [add_carry(): pl.pallas_call(functools.partial(carry_kernel, scale, steps, blocks), in_...]
    ppermute x6, starting transfers between devices: 11.8 us -> 11.2 us  [turn(): return lax.ppermute(x, 'seq', moves(lambda a: a, lambda b: (b + d) % NY))]
  transfers between devices with their start and end apart: 10 -> 10, of which waited for: 5 -> 6; matrix products, arithmetic and copies ran while one was open for 0% -> 0% of each run, Pallas kernels for 27% -> 23%
where the time goes in v2:
time: 46 us; the launch traced here: 45.7 us
  starting transfers between devices  18.4 us (40%)
  Pallas kernels  17.8 us (39%)
  waiting for transfers between devices  8.43 us (18%)
  between operations  0.91 us (2%)
    ppermute x6, starting transfers between devices, turn(): return lax.ppermute(x, 'seq', moves(lambda a: a, lambda b: (b + d) % NY))  11.2 us
    pallas_call x4, Pallas kernels, local_products(): pl.pallas_call(functools.partial(local_kernel, scale, h, blocks), in_spec...  8.2 us
    ppermute x4, starting transfers between devices, swap(): return lax.ppermute(x, 'seq', moves(zmap, lambda b: b))  7.24 us
    ppermute x4, waiting for transfers between devices, swap(): return lax.ppermute(x, 'seq', moves(zmap, lambda b: b))  6.73 us
    pallas_call x2, Pallas kernels, add_carry(): pl.pallas_call(functools.partial(carry_kernel, scale, steps, blocks), in_...  5.54 us
    pallas_call x1, Pallas kernels, device_sums(): pl.pallas_call(sums_kernel, in_specs=[SM] * 3 + [HB] * 4, out_specs=[VM]...  3.45 us
    ppermute x6, waiting for transfers between devices, turn(): return lax.ppermute(x, 'seq', moves(lambda a: a, lambda b: (b + d) % NY))  1.7 us
  transfers between devices with their start and end apart: 10, of which 6 were waited for; matrix products, arithmetic and copies ran while one was open for 0% of the time, Pallas kernels for 23%

profile of v2, /device:TPU:38, one launch (start us, length us, event | category | flops | bytes accessed | tf_op | source)
XLA Modules:
  0.0 45.7 jit_solution(7534802175234389181)
XLA Ops:
  0.6 3.5 %device_sums.1 = (bf16[1536,512]{1,0:T(8,128)(2,1)S(1)}, bf16[1536,512]{1,0:T(8,128)(2,1)S(1)}, bf16[1536,512]{1,0:T(8,128)(2,1)S(1)}, bf16[1536,512]{1,0:T(8,12...) custom-call(s32[1]{0:T(128)} %bitcast.me_ref, ...), custom_call_target="tpu_custom_call" | custom-call | tf_op jit(solution)/shard_map/device_sums/pallas_call | solution.py:95
  4.1 1.7 %collective-permute-start = (f32[256,128]{1,0:T(8,128)S(1)}, f32[256,128]{1,0:T(8,128)S(1)}, u32[]{:S(2)}, u32[]{:S(2)}) collective-permute-start(f32[256,128]{1,0:T(8,128)S(1)} %get-tuple-element.61), channel_id=1, source_target_pairs={{0,1},{1,2},{2,3},{3,0},{4,5},{5,6},{6,7},{7,4},{8,9},{9,10},{10,1... | collective-permute-start | bytes 393224 | tf_op jit(solution)/shard_map/ppermute | solution.py:266
  5.8 2.9 %collective-permute-start.1 = (f32[256,128]{1,0:T(8,128)S(1)}, f32[256,128]{1,0:T(8,128)S(1)}, u32[]{:S(2)}, u32[]{:S(2)}) collective-permute-start(f32[256,128]{1,0:T(8,128)S(1)} %get-tuple-element.62), channel_id=1, source_target_pairs={{0,2},{1,3},{2,0},{3,1},{4,6},{5,7},{6,4},{7,5},{8,10},{9,11},{10,... | collective-permute-start | bytes 393224 | tf_op jit(solution)/shard_map/ppermute | solution.py:266
  8.7 1.3 %collective-permute-start.2 = (f32[256,128]{1,0:T(8,128)S(1)}, f32[256,128]{1,0:T(8,128)S(1)}, u32[]{:S(2)}, u32[]{:S(2)}) collective-permute-start(f32[256,128]{1,0:T(8,128)S(1)} %get-tuple-element.63), channel_id=1, source_target_pairs={{0,3},{1,0},{2,1},{3,2},{4,7},{5,4},{6,5},{7,6},{8,11},{9,8},{10,9... | collective-permute-start | bytes 393224 | tf_op jit(solution)/shard_map/ppermute | solution.py:266
  10.0 2.1 %local_products.4 = (f32[1536,512]{1,0:T(8,128)S(1)}, f32[1536,512]{1,0:T(8,128)S(1)}, f32[1536,512]{1,0:T(8,128)S(1)}, f32[1536,512]{1,0:T(8,128)S(1)}) custom-call(bf16[1536,512]{1,0:T(8,128)(2,1)S(1)} %get-tuple-element.38.q_ref.q.refs_0_, bf16[1536,512]{1,0:T(8,128)(2,1)S(1)} %get-tuple-element.39.k_ref.k.refs_1_, ...), custom_call_target="tpu_custom_call" | custom-call | flops 2000000000 | bytes 1024 | tf_op jit(solution)/shard_map/local_products/pallas_call | solution.py:160
  12.1 0.4 own_sums.1
  12.5 2.1 %local_products.5 = (f32[1536,512]{1,0:T(8,128)S(1)}, f32[1536,512]{1,0:T(8,128)S(1)}, f32[1536,512]{1,0:T(8,128)S(1)}, f32[1536,512]{1,0:T(8,128)S(1)}) custom-call(bf16[1536,512]{1,0:T(8,128)(2,1)S(1)} %get-tuple-element.38.q_ref.q.refs_0_, ...), custom_call_target="tpu_custom_call", output_to_operand_aliasing={{0}: (4, {}), {1}: (5, {}), {2}: (6, {}), {3}: (7, {})} | custom-call | flops 2000000000 | bytes 1024 | tf_op jit(solution)/shard_map/local_products/pallas_call | solution.py:160
  14.5 0.0 collective-permute-done.g1
  14.6 0.1 collective-permute-done.1.g2
  14.7 0.0 collective-permute-done.2.g3
  14.7 0.2 collective-permute-start.3
  14.9 2.0 %local_products.6 = (f32[1536,512]{1,0:T(8,128)S(1)}, f32[1536,512]{1,0:T(8,128)S(1)}, f32[1536,512]{1,0:T(8,128)S(1)}, f32[1536,512]{1,0:T(8,128)S(1)}) custom-call(bf16[1536,512]{1,0:T(8,128)(2,1)S(1)} %get-tuple-element.38.q_ref.q.refs_0_, ...), custom_call_target="tpu_custom_call", output_to_operand_aliasing={{0}: (4, {}), {1}: (5, {}), {2}: (6, {}), {3}: (7, {})} | custom-call | flops 2000000000 | bytes 1024 | tf_op jit(solution)/shard_map/local_products/pallas_call | solution.py:160
  17.0 2.8 %collective-permute-done.3.pair = f32[256,128]{1,0:T(8,128)S(1)} collective-permute-done((f32[256,128]{1,0:T(8,128)S(1)}, f32[256,128]{1,0:T(8,128)S(1)}, u32[]{:S(2)}, u32[]{:S(2)}) %collective-permute-start.3) | collective-permute-done | bytes 131104 | tf_op jit(solution)/shard_map/ppermute | solution.py:263
  19.8 5.9 %collective-permute-start.5 = (f32[128,128]{1,0:T(8,128)S(1)}, f32[128,128]{1,0:T(8,128)S(1)}, u32[]{:S(2)}, u32[]{:S(2)}) collective-permute-start(f32[128,128]{1,0:T(8,128)S(1)} %get-tuple-element.78), channel_id=1, source_target_pairs={{0,20},{1,21},{2,22},{3,23},{4,16},{5,17},{6,18},{7,19},{8,28},{9,... | collective-permute-start | bytes 196616 | tf_op jit(solution)/shard_map/ppermute | solution.py:263
  25.7 1.0 %collective-permute-start.6 = (f32[128,128]{1,0:T(8,128)S(1)}, f32[128,128]{1,0:T(8,128)S(1)}, u32[]{:S(2)}, u32[]{:S(2)}) collective-permute-start(f32[128,128]{1,0:T(8,128)S(1)} %get-tuple-element.78), channel_id=1, source_target_pairs={{0,28},{1,29},{2,30},{3,31},{4,24},{5,25},{6,26},{7,27},{8,20},{9,... | collective-permute-start | bytes 196616 | tf_op jit(solution)/shard_map/ppermute | solution.py:263
  26.7 0.1 collective-permute-start.4
  26.8 2.0 %local_products.7 = (f32[1536,512]{1,0:T(8,128)S(1)}, f32[1536,512]{1,0:T(8,128)S(1)}, f32[1536,512]{1,0:T(8,128)S(1)}, f32[1536,512]{1,0:T(8,128)S(1)}) custom-call(bf16[1536,512]{1,0:T(8,128)(2,1)S(1)} %get-tuple-element.38.q_ref.q.refs_0_, ...), custom_call_target="tpu_custom_call", output_to_operand_aliasing={{0}: (4, {}), {1}: (5, {}), {2}: (6, {}), {3}: (7, {})} | custom-call | flops 2000000000 | bytes 1024 | tf_op jit(solution)/shard_map/local_products/pallas_call | solution.py:160
  28.9 0.2 make_ready.1
  29.1 2.6 %collective-permute-done.4 = f32[128,128]{1,0:T(8,128)S(1)} collective-permute-done((f32[128,128]{1,0:T(8,128)S(1)}, f32[128,128]{1,0:T(8,128)S(1)}, u32[]{:S(2)}, u32[]{:S(2)}) %collective-permute-start.4) | collective-permute-done | bytes 65568 | tf_op jit(solution)/shard_map/ppermute | solution.py:263
  31.7 0.0 collective-permute-done.5
  31.7 1.3 %collective-permute-done.6 = f32[128,128]{1,0:T(8,128)S(1)} collective-permute-done((f32[128,128]{1,0:T(8,128)S(1)}, f32[128,128]{1,0:T(8,128)S(1)}, u32[]{:S(2)}, u32[]{:S(2)}) %collective-permute-start.6) | collective-permute-done | bytes 65568 | tf_op jit(solution)/shard_map/ppermute | solution.py:263
  33.1 1.3 %collective-permute-start.7 = (f32[256,128]{1,0:T(8,128)S(1)}, f32[256,128]{1,0:T(8,128)S(1)}, u32[]{:S(2)}, u32[]{:S(2)}) collective-permute-start(f32[256,128]{1,0:T(8,128)S(1)} %get-tuple-element.77), channel_id=1, source_target_pairs={{0,1},{1,2},{2,3},{3,0},{4,5},{5,6},{6,7},{7,4},{8,9},{9,10},{10,1... | collective-permute-start | bytes 393224 | tf_op jit(solution)/shard_map/ppermute | solution.py:266
  34.4 2.4 %collective-permute-start.8 = (f32[256,128]{1,0:T(8,128)S(1)}, f32[256,128]{1,0:T(8,128)S(1)}, u32[]{:S(2)}, u32[]{:S(2)}) collective-permute-start(f32[256,128]{1,0:T(8,128)S(1)} %get-tuple-element.75), channel_id=1, source_target_pairs={{0,2},{1,3},{2,0},{3,1},{4,6},{5,7},{6,4},{7,5},{8,10},{9,11},{10,... | collective-permute-start | bytes 393224 | tf_op jit(solution)/shard_map/ppermute | solution.py:266
  36.8 1.6 %collective-permute-start.9 = (f32[256,128]{1,0:T(8,128)S(1)}, f32[256,128]{1,0:T(8,128)S(1)}, u32[]{:S(2)}, u32[]{:S(2)}) collective-permute-start(f32[256,128]{1,0:T(8,128)S(1)} %get-tuple-element.76), channel_id=1, source_target_pairs={{0,3},{1,0},{2,1},{3,2},{4,7},{5,4},{6,5},{7,6},{8,11},{9,8},{10,9... | collective-permute-start | bytes 393224 | tf_op jit(solution)/shard_map/ppermute | solution.py:266
  38.4 1.8 %add_carry.2 = (bf16[1536,512]{1,0:T(8,128)(2,1)}, bf16[1536,512]{1,0:T(8,128)(2,1)}, bf16[1536,512]{1,0:T(8,128)(2,1)}, bf16[1536,512]{1,0:T(8,128)(2,1)}) custom-call(s32[1]{0:T(128)} %bitcast.me_ref, bf16[1536,512]{1,0:T(8,128)(2,1)S(1)} %get-tuple-element.38.q_ref.q.refs_0_, bf16[1536,512]{1,0:T(8,128)(2,1)S(1)} %get-tuple-element.39.k_ref.k.refs_1_, ...), custom_call_target="tpu_custom_call" | custom-call | flops 1500000000 | bytes 1024 | tf_op jit(solution)/shard_map/add_carry/pallas_call | solution.py:237
  40.2 0.0 collective-permute-done.7.refs_10_
  40.2 1.0 %collective-permute-done.8.refs_11_ = f32[256,128]{1,0:T(8,128)S(1)} collective-permute-done((f32[256,128]{1,0:T(8,128)S(1)}, f32[256,128]{1,0:T(8,128)S(1)}, u32[]{:S(2)}, u32[]{:S(2)}) %collective-permute-start.8) | collective-permute-done | bytes 131104 | tf_op jit(solution)/shard_map/ppermute | solution.py:266
  41.1 0.6 %collective-permute-done.9.refs_12_ = f32[256,128]{1,0:T(8,128)S(1)} collective-permute-done((f32[256,128]{1,0:T(8,128)S(1)}, f32[256,128]{1,0:T(8,128)S(1)}, u32[]{:S(2)}, u32[]{:S(2)}) %collective-permute-start.9) | collective-permute-done | bytes 131104 | tf_op jit(solution)/shard_map/ppermute | solution.py:266
  41.7 3.7 %add_carry.3 = (bf16[1536,512]{1,0:T(8,128)(2,1)}, bf16[1536,512]{1,0:T(8,128)(2,1)}, bf16[1536,512]{1,0:T(8,128)(2,1)}, bf16[1536,512]{1,0:T(8,128)(2,1)}) custom-call(s32[1]{0:T(128)} %bitcast.me_ref, bf16[1536,512]{1,0:T(8,128)(2,1)S(1)} %get-tuple-element.38.q_ref.q.refs_0_, ...), custom_call_target="tpu_custom_call", output_to_operand_aliasing={{0}: (14, {}), {1}: (15, {}), {2}: (16, {}), {3}: (17, {})} | custom-call | flops 4499999744 | bytes 1024 | tf_op jit(solution)/shard_map/add_carry/pallas_call | solution.py:237
  (5 shorter events, 0.1 us)
Async XLA Ops:
  4.1 10.5 %collective-permute-start = (f32[256,128]{1,0:T(8,128)S(1)}, f32[256,128]{1,0:T(8,128)S(1)}, u32[]{:S(2)}, u32[]{:S(2)}) collective-permute-start(f32[256,128]{1,0:T(8,128)S(1)} %get-tuple-element.61), channel_id=1, source_target_pairs={{0,1},{1,2},{2,3},{3,0},{4,5},{5,6},{6,7},{7,4},{8,9},{9,10},{10,1... | collective-permute-start | bytes 393224 | tf_op jit(solution)/shard_map/ppermute | solution.py:266
  5.8 8.9 %collective-permute-start.1 = (f32[256,128]{1,0:T(8,128)S(1)}, f32[256,128]{1,0:T(8,128)S(1)}, u32[]{:S(2)}, u32[]{:S(2)}) collective-permute-start(f32[256,128]{1,0:T(8,128)S(1)} %get-tuple-element.62), channel_id=1, source_target_pairs={{0,2},{1,3},{2,0},{3,1},{4,6},{5,7},{6,4},{7,5},{8,10},{9,11},{10,... | collective-permute-start | bytes 393224 | tf_op jit(solution)/shard_map/ppermute | solution.py:266
  8.7 6.0 %collective-permute-start.2 = (f32[256,128]{1,0:T(8,128)S(1)}, f32[256,128]{1,0:T(8,128)S(1)}, u32[]{:S(2)}, u32[]{:S(2)}) collective-permute-start(f32[256,128]{1,0:T(8,128)S(1)} %get-tuple-element.63), channel_id=1, source_target_pairs={{0,3},{1,0},{2,1},{3,2},{4,7},{5,4},{6,5},{7,6},{8,11},{9,8},{10,9... | collective-permute-start | bytes 393224 | tf_op jit(solution)/shard_map/ppermute | solution.py:266
  14.7 5.1 %collective-permute-start.3 = (f32[256,128]{1,0:T(8,128)S(1)}, f32[256,128]{1,0:T(8,128)S(1)}, u32[]{:S(2)}, u32[]{:S(2)}) collective-permute-start(f32[256,128]{1,0:T(8,128)S(1)} %add_add_fusion), channel_id=1, source_target_pairs={{0,4},{1,5},{2,6},{3,7},{4,0},{5,1},{6,2},{7,3},{8,12},{9,13},{10,... | collective-permute-start | bytes 393224 | tf_op jit(solution)/shard_map/ppermute | solution.py:263
  19.8 11.9 %collective-permute-start.5 = (f32[128,128]{1,0:T(8,128)S(1)}, f32[128,128]{1,0:T(8,128)S(1)}, u32[]{:S(2)}, u32[]{:S(2)}) collective-permute-start(f32[128,128]{1,0:T(8,128)S(1)} %get-tuple-element.78), channel_id=1, source_target_pairs={{0,20},{1,21},{2,22},{3,23},{4,16},{5,17},{6,18},{7,19},{8,28},{9,... | collective-permute-start | bytes 196616 | tf_op jit(solution)/shard_map/ppermute | solution.py:263
  25.7 7.3 %collective-permute-start.6 = (f32[128,128]{1,0:T(8,128)S(1)}, f32[128,128]{1,0:T(8,128)S(1)}, u32[]{:S(2)}, u32[]{:S(2)}) collective-permute-start(f32[128,128]{1,0:T(8,128)S(1)} %get-tuple-element.78), channel_id=1, source_target_pairs={{0,28},{1,29},{2,30},{3,31},{4,24},{5,25},{6,26},{7,27},{8,20},{9,... | collective-permute-start | bytes 196616 | tf_op jit(solution)/shard_map/ppermute | solution.py:263
  26.7 5.0 %collective-permute-start.4 = (f32[128,128]{1,0:T(8,128)S(1)}, f32[128,128]{1,0:T(8,128)S(1)}, u32[]{:S(2)}, u32[]{:S(2)}) collective-permute-start(f32[128,128]{1,0:T(8,128)S(1)} %get-tuple-element.79), channel_id=1, source_target_pairs={{0,12},{1,13},{2,14},{3,15},{4,8},{5,9},{6,10},{7,11},{8,4},{9,5},... | collective-permute-start | bytes 196616 | tf_op jit(solution)/shard_map/ppermute | solution.py:263
  33.1 7.1 %collective-permute-start.7 = (f32[256,128]{1,0:T(8,128)S(1)}, f32[256,128]{1,0:T(8,128)S(1)}, u32[]{:S(2)}, u32[]{:S(2)}) collective-permute-start(f32[256,128]{1,0:T(8,128)S(1)} %get-tuple-element.77), channel_id=1, source_target_pairs={{0,1},{1,2},{2,3},{3,0},{4,5},{5,6},{6,7},{7,4},{8,9},{9,10},{10,1... | collective-permute-start | bytes 393224 | tf_op jit(solution)/shard_map/ppermute | solution.py:266
  34.4 6.7 %collective-permute-start.8 = (f32[256,128]{1,0:T(8,128)S(1)}, f32[256,128]{1,0:T(8,128)S(1)}, u32[]{:S(2)}, u32[]{:S(2)}) collective-permute-start(f32[256,128]{1,0:T(8,128)S(1)} %get-tuple-element.75), channel_id=1, source_target_pairs={{0,2},{1,3},{2,0},{3,1},{4,6},{5,7},{6,4},{7,5},{8,10},{9,11},{10,... | collective-permute-start | bytes 393224 | tf_op jit(solution)/shard_map/ppermute | solution.py:266
  36.8 5.0 %collective-permute-start.9 = (f32[256,128]{1,0:T(8,128)S(1)}, f32[256,128]{1,0:T(8,128)S(1)}, u32[]{:S(2)}, u32[]{:S(2)}) collective-permute-start(f32[256,128]{1,0:T(8,128)S(1)} %get-tuple-element.76), channel_id=1, source_target_pairs={{0,3},{1,0},{2,1},{3,2},{4,7},{5,4},{6,5},{7,6},{8,11},{9,8},{10,9... | collective-permute-start | bytes 393224 | tf_op jit(solution)/shard_map/ppermute | solution.py:266

commit v3 on v2

--- a/solution.py
+++ b/solution.py
@@ -18,8 +18,11 @@
 F32 = jnp.float32
 BF16 = jnp.bfloat16
 VM = pl.BlockSpec(memory_space=pltpu.VMEM)
-SM = pl.BlockSpec(memory_space=pltpu.SMEM)
 HB = pl.BlockSpec(memory_space=pltpu.HBM)
+
+
+def side():
+    return 1 - 2 * (lax.axis_index("dp") & 1)
 
 
 def dot(a, b, ca, cb):
@@ -43,9 +46,9 @@
 CHUNKS = ((0, 512), (512, 512), (1024, 256), (1280, 256))
 
 
-def head_sums(me_ref, xs, d, out, cum):
+def head_sums(xs, d, out, cum):
     q, k, v, g = xs
-    cols = pl.ds(pl.multiple_of(((me_ref[0] + d) & 3) * DH, DH), DH)
+    cols = pl.ds(pl.multiple_of(((lax.axis_index("seq") + side() * d) & 3) * DH, DH), DH)
     state = {"kv": 0.0, "first": 0.0}
 
     def step(n):
@@ -70,8 +73,8 @@
     return step, finish
 
 
-def sums_kernel(me_ref, high_ref, up_ref, *refs):
-    srcs, dsts, outs, cum, sems = refs[:4], refs[4:8], refs[8:11], refs[11], refs[12]
+def sums_kernel(*refs):
+    srcs, dsts, outs, cum, high, up, sems = refs[:4], refs[4:8], refs[8:11], refs[11], refs[12], refs[13], refs[14]
     copies = []
     for n, (start, size) in enumerate(CHUNKS):
         rows = pl.ds(start, size)
@@ -79,7 +82,10 @@
     for row in copies:
         for c in row:
             c.start()
-    heads = [head_sums(me_ref, dsts, d + 1, outs[d], cum.at[d]) for d in range(3)]
+    z = lax.axis_index("seq") >> 2
+    high[...] = jnp.full(high.shape, z >> 2, jnp.int32).astype(F32)
+    up[...] = jnp.full(up.shape, (z >> 1) & 1, jnp.int32).astype(F32)
+    heads = [head_sums(dsts, d + 1, outs[d], cum.at[d]) for d in range(3)]
     for n in range(len(CHUNKS)):
         for c in copies[n]:
             c.wait()
@@ -89,38 +95,39 @@
         finish()
 
 
-def device_sums(me, high, up, q, k, v, g):
+def device_sums(q, k, v, g):
     rows, width = q.shape
     one = jax.ShapeDtypeStruct((2 * DH, DH), F32)
     return pl.pallas_call(
         sums_kernel,
-        in_specs=[SM] * 3 + [HB] * 4,
-        out_specs=[VM] * 8,
-        out_shape=[pltpu.VMEM((rows, width), BF16)] * 4 + [one] * 3 + [pltpu.VMEM((3, rows // SPAN - 1, 2 * DH, DH), F32)],
+        in_specs=[HB] * 4,
+        out_specs=[VM] * 10,
+        out_shape=[pltpu.VMEM((rows, width), BF16)] * 4 + [one] * 3 + [pltpu.VMEM((3, rows // SPAN - 1, 2 * DH, DH), F32)]
+        + [jax.ShapeDtypeStruct((DH, DH), F32)] * 2,
         scratch_shapes=[pltpu.SemaphoreType.DMA((len(CHUNKS), 4))],
         compiler_params=pltpu.CompilerParams(vmem_limit_bytes=16 * 2**20),
         name="device_sums",
-    )(me, high, up, q, k, v, g)
-
-
-def own_kernel(me_ref, q, k, v, g, out, cum):
-    step, finish = head_sums(me_ref, (q, k, v, g), 0, out, cum.at[0])
+    )(q, k, v, g)
+
+
+def own_kernel(q, k, v, g, out, cum):
+    step, finish = head_sums((q, k, v, g), 0, out, cum.at[0])
     for n in range(len(CHUNKS)):
         step(n)
     finish()
 
 
-def own_sums(me, xs):
+def own_sums(xs):
     rows = xs[0].shape[0]
     return pl.pallas_call(
         own_kernel,
-        in_specs=[SM] + [VM] * 4,
+        in_specs=[VM] * 4,
         out_specs=[VM] * 2,
         out_shape=[jax.ShapeDtypeStruct((2 * DH, DH), F32), pltpu.VMEM((1, rows // SPAN - 1, 2 * DH, DH), F32)],
         compiler_params=pltpu.CompilerParams(vmem_limit_bytes=8 * 2**20),
         cost_estimate=pl.CostEstimate(flops=100_000_000, bytes_accessed=1024, transcendentals=0),
         name="own_sums",
-    )(me, *xs)
+    )(*xs)
 
 
 def local_kernel(scale, h, blocks, q_ref, k_ref, v_ref, g_ref, *refs):
@@ -169,8 +176,8 @@
     )(*xs, *parts)
 
 
-def ready_kernel(me_ref, g0, g1, g2, g3, pair, *outs):
-    y, z = me_ref[0] & 3, me_ref[0] >> 2
+def ready_kernel(g0, g1, g2, g3, pair, *outs):
+    y, z, way = lax.axis_index("seq") & 3, lax.axis_index("seq") >> 2, side()
     got = [(r[:DH], r[DH:]) for r in (g0, g1, g2, g3)]
 
     def when(c, x):
@@ -179,34 +186,34 @@
     kv = when((z & 1) != 0, pair[:DH])
     qg = when((z & 1) == 0, pair[DH:])
     for e, out in enumerate(outs):
-        dst = (y + e) & 3
+        dst = (y + way * e) & 3
         a, b = kv, qg
         for d in range(NY):
-            src = (y - d) & 3
+            src = (y - way * d) & 3
             a = a + when(src < dst, got[d][0])
             b = b + when(src > dst, got[d][1])
         out[:DH] = a
         out[DH:] = b
 
 
-def make_ready(me, *arrays):
+def make_ready(*arrays):
     return pl.pallas_call(
         ready_kernel,
-        in_specs=[SM] + [VM] * len(arrays),
+        in_specs=[VM] * len(arrays),
         out_specs=[VM] * NY,
         out_shape=[jax.ShapeDtypeStruct((2 * DH, DH), F32)] * NY,
         compiler_params=pltpu.CompilerParams(vmem_limit_bytes=8 * 2**20),
         name="make_ready",
-    )(me, *arrays)
-
-
-def carry_kernel(scale, steps, blocks, me_ref, *refs):
+    )(*arrays)
+
+
+def carry_kernel(scale, steps, blocks, *refs):
     xs, parts, cums, refs = refs[:4], refs[4:8], refs[8:10], refs[10:]
     priors, outs, stage, sems = refs[: len(steps)], refs[-6:-2], refs[-2], refs[-1]
     q, k, v, g = xs
     copies = []
     for i, (d, prior) in enumerate(zip(steps, priors)):
-        h = (me_ref[0] - d) & 3
+        h = (lax.axis_index("seq") - side() * d) & 3
         cols = pl.ds(pl.multiple_of(h * DH, DH), DH)
         cum = cums[1].at[HEADS - 1 - d] if d else cums[0].at[0]
         for n in range(blocks):
@@ -230,21 +237,21 @@
         copy.wait()
 
 
-def add_carry(scale, me, steps, xs, parts, cums, priors, before):
+def add_carry(scale, steps, xs, parts, cums, priors, before):
     rows, width = xs[0].shape
     blocks = rows // SPAN
     m = len(steps)
     return pl.pallas_call(
         functools.partial(carry_kernel, scale, steps, blocks),
-        in_specs=[SM] + [VM] * (10 + m) + [HB] * len(before),
+        in_specs=[VM] * (10 + m) + [HB] * len(before),
         out_specs=[HB] * 4,
         out_shape=[pltpu.HBM((rows, width), BF16)] * 4,
-        input_output_aliases={11 + m + i: i for i in range(len(before))},
+        input_output_aliases={10 + m + i: i for i in range(len(before))},
         scratch_shapes=[pltpu.VMEM((m, 4, rows, DH), BF16), pltpu.SemaphoreType.DMA((m, 4, blocks + 1))],
         compiler_params=pltpu.CompilerParams(vmem_limit_bytes=16 * 2**20),
         cost_estimate=pl.CostEstimate(flops=m * 1_500_000_000, bytes_accessed=1024, transcendentals=0),
         name="add_carry",
-    )(me, *xs, *parts, *cums, *priors, *before)
+    )(*xs, *parts, *cums, *priors, *before)
 
 
 def moves(zmap, ymap):
@@ -255,22 +262,25 @@
     rows = query.shape[0]
     scale = 1.0 / math.sqrt(DH * rows * lax.axis_size("seq"))
     blocks = rows // SPAN
-    index = lax.axis_index("seq")
-    me = index.reshape(1)
     inputs = [pltpu.with_memory_space_constraint(x, pltpu.HBM) for x in (query, key_in, value, grad_out)]
 
     def swap(x, zmap):
         return lax.ppermute(x, "seq", moves(zmap, lambda b: b))
 
     def turn(x, d):
-        return lax.ppermute(x, "seq", moves(lambda a: a, lambda b: (b + d) % NY))
-
-    high, up = index >= NY * NZ // 2, (index & (2 * NY)) != 0
-    flags = [c.astype(jnp.int32).reshape(1) for c in (high, up)]
-    q, k, v, g, *own, others = device_sums(me, *flags, *inputs)
+        ring = NY * NZ
+        pairs = [
+            (p * ring + i, p * ring + j)
+            for p in range(lax.axis_size("dp"))
+            for i, j in moves(lambda a: a, lambda b: (b + (1 - 2 * (p & 1)) * d) % NY)
+        ]
+        return lax.ppermute(x, ("dp", "seq"), pairs)
+
+    q, k, v, g, *own, others, high, up = device_sums(*inputs)
     xs = (q, k, v, g)
+    high, up = high > 0.5, up > 0.5
     sent = [turn(own[d - 1], d) for d in range(1, NY)]
-    mine, inner = own_sums(me, xs)
+    mine, inner = own_sums(xs)
     got = [mine] + sent
     parts = ()
     for h in range(HEADS):
@@ -289,11 +299,11 @@
         ],
         axis=0,
     )
-    ready = [x + last for x in make_ready(me, *got, pair)]
+    ready = [x + last for x in make_ready(*got, pair)]
     prior = {0: ready[0]} | {d: turn(ready[d], d) for d in (2, 3, 1)}
     outs = ()
     for steps in ((0,), (1, 2, 3)):
-        outs = add_carry(scale, me, steps, xs, parts, (inner, others), [prior[d] for d in steps], outs)
+        outs = add_carry(scale, steps, xs, parts, (inner, others), [prior[d] for d in steps], outs)
     return tuple(outs)
 
 

time: 46 us -> 46.8 us (1.017)
  waiting for transfers between devices: 8.43 us -> 10.8 us
  starting transfers between devices: 18.4 us -> 17.3 us
    ppermute x6, waiting for transfers between devices: 1.7 us -> 3.59 us  [turn(): return lax.ppermute(x, ('dp', 'seq'), pairs)]
    ppermute x6, starting transfers between devices: 11.2 us -> 10.1 us  [turn(): return lax.ppermute(x, ('dp', 'seq'), pairs)]
  transfers between devices with their start and end apart: 10 -> 10, of which waited for: 6 -> 6; matrix products, arithmetic and copies ran while one was open for 0% -> 0% of each run, Pallas kernels for 23% -> 22%
where the time goes in v3:
time: 46.8 us
  Pallas kernels  17.6 us (38%)
  starting transfers between devices  17.3 us (37%)
  waiting for transfers between devices  10.8 us (23%)
  between operations  0.9 us (2%)
    ppermute x6, starting transfers between devices, turn(): return lax.ppermute(x, ('dp', 'seq'), pairs)  10.1 us
    pallas_call x4, Pallas kernels, local_products(): pl.pallas_call(functools.partial(local_kernel, scale, h, blocks), in_spec...  8.06 us
    ppermute x4, starting transfers between devices, swap(): return lax.ppermute(x, 'seq', moves(zmap, lambda b: b))  7.24 us
    ppermute x4, waiting for transfers between devices, swap(): return lax.ppermute(x, 'seq', moves(zmap, lambda b: b))  7.2 us
    pallas_call x2, Pallas kernels, add_carry(): pl.pallas_call(functools.partial(carry_kernel, scale, steps, blocks), in_...  5.54 us
    ppermute x6, waiting for transfers between devices, turn(): return lax.ppermute(x, ('dp', 'seq'), pairs)  3.59 us
    pallas_call x1, Pallas kernels, device_sums(): pl.pallas_call(sums_kernel, in_specs=[HB] * 4, out_specs=[VM] * 10, out_s...  3.44 us
  transfers between devices with their start and end apart: 10, of which 6 were waited for; matrix products, arithmetic and copies ran while one was open for 0% of the time, Pallas kernels for 22%

profile of v3, /device:TPU:38, one launch (start us, length us, event | category | flops | bytes accessed | tf_op | source)
XLA Modules:
  0.0 46.8 jit_solution(15800310153748282112)
XLA Ops:
  0.6 3.4 %device_sums.1 = (bf16[1536,512]{1,0:T(8,128)(2,1)S(1)}, bf16[1536,512]{1,0:T(8,128)(2,1)S(1)}, bf16[1536,512]{1,0:T(8,128)(2,1)S(1)}, bf16[1536,512]{1,0:T(8,12...) custom-call(bf16[1536,512]{1,0:T(8,128)(2,1)} %refs_0_.1, ...), custom_call_target="tpu_custom_call" | custom-call | tf_op jit(solution)/shard_map/device_sums/pallas_call | solution.py:101
  4.1 1.7 %collective-permute-start = (f32[256,128]{1,0:T(8,128)S(1)}, f32[256,128]{1,0:T(8,128)S(1)}, u32[]{:S(2)}, u32[]{:S(2)}) collective-permute-start(f32[256,128]{1,0:T(8,128)S(1)} %get-tuple-element.63), channel_id=1, source_target_pairs={{0,1},{1,2},{2,3},{3,0},{4,5},{5,6},{6,7},{7,4},{8,9},{9,10},{10,1... | collective-permute-start | bytes 393224 | tf_op jit(solution)/shard_map/ppermute | solution.py:277
  5.7 2.9 %collective-permute-start.1 = (f32[256,128]{1,0:T(8,128)S(1)}, f32[256,128]{1,0:T(8,128)S(1)}, u32[]{:S(2)}, u32[]{:S(2)}) collective-permute-start(f32[256,128]{1,0:T(8,128)S(1)} %get-tuple-element.64), channel_id=1, source_target_pairs={{0,2},{1,3},{2,0},{3,1},{4,6},{5,7},{6,4},{7,5},{8,10},{9,11},{10,... | collective-permute-start | bytes 393224 | tf_op jit(solution)/shard_map/ppermute | solution.py:277
  8.6 1.3 %collective-permute-start.2 = (f32[256,128]{1,0:T(8,128)S(1)}, f32[256,128]{1,0:T(8,128)S(1)}, u32[]{:S(2)}, u32[]{:S(2)}) collective-permute-start(f32[256,128]{1,0:T(8,128)S(1)} %get-tuple-element.65), channel_id=1, source_target_pairs={{0,3},{1,0},{2,1},{3,2},{4,7},{5,4},{6,5},{7,6},{8,11},{9,8},{10,9... | collective-permute-start | bytes 393224 | tf_op jit(solution)/shard_map/ppermute | solution.py:277
  10.0 2.0 %local_products.4 = (f32[1536,512]{1,0:T(8,128)S(1)}, f32[1536,512]{1,0:T(8,128)S(1)}, f32[1536,512]{1,0:T(8,128)S(1)}, f32[1536,512]{1,0:T(8,128)S(1)}) custom-call(bf16[1536,512]{1,0:T(8,128)(2,1)S(1)} %get-tuple-element.40.q_ref.q.refs_0_, bf16[1536,512]{1,0:T(8,128)(2,1)S(1)} %get-tuple-element.41.k_ref.k.refs_1_, ...), custom_call_target="tpu_custom_call" | custom-call | flops 2000000000 | bytes 1024 | tf_op jit(solution)/shard_map/local_products/pallas_call | solution.py:167
  12.0 0.4 own_sums.1
  12.4 2.0 %local_products.5 = (f32[1536,512]{1,0:T(8,128)S(1)}, f32[1536,512]{1,0:T(8,128)S(1)}, f32[1536,512]{1,0:T(8,128)S(1)}, f32[1536,512]{1,0:T(8,128)S(1)}) custom-call(bf16[1536,512]{1,0:T(8,128)(2,1)S(1)} %get-tuple-element.40.q_ref.q.refs_0_, ...), custom_call_target="tpu_custom_call", output_to_operand_aliasing={{0}: (4, {}), {1}: (5, {}), {2}: (6, {}), {3}: (7, {})} | custom-call | flops 2000000000 | bytes 1024 | tf_op jit(solution)/shard_map/local_products/pallas_call | solution.py:167
  14.5 0.0 collective-permute-done.g1
  14.5 0.8 %collective-permute-done.1.g2 = f32[256,128]{1,0:T(8,128)S(1)} collective-permute-done((f32[256,128]{1,0:T(8,128)S(1)}, f32[256,128]{1,0:T(8,128)S(1)}, u32[]{:S(2)}, u32[]{:S(2)}) %collective-permute-start.1) | collective-permute-done | bytes 131104 | tf_op jit(solution)/shard_map/ppermute | solution.py:277
  15.2 0.0 collective-permute-done.2.g3
  15.3 0.2 collective-permute-start.3
  15.5 2.0 %local_products.6 = (f32[1536,512]{1,0:T(8,128)S(1)}, f32[1536,512]{1,0:T(8,128)S(1)}, f32[1536,512]{1,0:T(8,128)S(1)}, f32[1536,512]{1,0:T(8,128)S(1)}) custom-call(bf16[1536,512]{1,0:T(8,128)(2,1)S(1)} %get-tuple-element.40.q_ref.q.refs_0_, ...), custom_call_target="tpu_custom_call", output_to_operand_aliasing={{0}: (4, {}), {1}: (5, {}), {2}: (6, {}), {3}: (7, {})} | custom-call | flops 2000000000 | bytes 1024 | tf_op jit(solution)/shard_map/local_products/pallas_call | solution.py:167
  17.5 3.0 %collective-permute-done.3.pair = f32[256,128]{1,0:T(8,128)S(1)} collective-permute-done((f32[256,128]{1,0:T(8,128)S(1)}, f32[256,128]{1,0:T(8,128)S(1)}, u32[]{:S(2)}, u32[]{:S(2)}) %collective-permute-start.3) | collective-permute-done | bytes 131104 | tf_op jit(solution)/shard_map/ppermute | solution.py:268
  20.5 5.9 %collective-permute-start.5 = (f32[128,128]{1,0:T(8,128)S(1)}, f32[128,128]{1,0:T(8,128)S(1)}, u32[]{:S(2)}, u32[]{:S(2)}) collective-permute-start(f32[128,128]{1,0:T(8,128)S(1)} %get-tuple-element.86), channel_id=1, source_target_pairs={{0,20},{1,21},{2,22},{3,23},{4,16},{5,17},{6,18},{7,19},{8,28},{9,... | collective-permute-start | bytes 196616 | tf_op jit(solution)/shard_map/ppermute | solution.py:268
  26.5 1.0 %collective-permute-start.6 = (f32[128,128]{1,0:T(8,128)S(1)}, f32[128,128]{1,0:T(8,128)S(1)}, u32[]{:S(2)}, u32[]{:S(2)}) collective-permute-start(f32[128,128]{1,0:T(8,128)S(1)} %get-tuple-element.86), channel_id=1, source_target_pairs={{0,28},{1,29},{2,30},{3,31},{4,24},{5,25},{6,26},{7,27},{8,20},{9,... | collective-permute-start | bytes 196616 | tf_op jit(solution)/shard_map/ppermute | solution.py:268
  27.5 0.1 collective-permute-start.4
  27.6 2.0 %local_products.7 = (f32[1536,512]{1,0:T(8,128)S(1)}, f32[1536,512]{1,0:T(8,128)S(1)}, f32[1536,512]{1,0:T(8,128)S(1)}, f32[1536,512]{1,0:T(8,128)S(1)}) custom-call(bf16[1536,512]{1,0:T(8,128)(2,1)S(1)} %get-tuple-element.40.q_ref.q.refs_0_, ...), custom_call_target="tpu_custom_call", output_to_operand_aliasing={{0}: (4, {}), {1}: (5, {}), {2}: (6, {}), {3}: (7, {})} | custom-call | flops 2000000000 | bytes 1024 | tf_op jit(solution)/shard_map/local_products/pallas_call | solution.py:167
  29.6 0.2 make_ready.1
  29.8 2.2 %collective-permute-done.4 = f32[128,128]{1,0:T(8,128)S(1)} collective-permute-done((f32[128,128]{1,0:T(8,128)S(1)}, f32[128,128]{1,0:T(8,128)S(1)}, u32[]{:S(2)}, u32[]{:S(2)}) %collective-permute-start.4) | collective-permute-done | bytes 65568 | tf_op jit(solution)/shard_map/ppermute | solution.py:268
  32.0 0.0 collective-permute-done.5
  32.0 2.0 %collective-permute-done.6 = f32[128,128]{1,0:T(8,128)S(1)} collective-permute-done((f32[128,128]{1,0:T(8,128)S(1)}, f32[128,128]{1,0:T(8,128)S(1)}, u32[]{:S(2)}, u32[]{:S(2)}) %collective-permute-start.6) | collective-permute-done | bytes 65568 | tf_op jit(solution)/shard_map/ppermute | solution.py:268
  34.1 0.1 collective-permute-start.7
  34.1 2.9 %collective-permute-start.8 = (f32[256,128]{1,0:T(8,128)S(1)}, f32[256,128]{1,0:T(8,128)S(1)}, u32[]{:S(2)}, u32[]{:S(2)}) collective-permute-start(f32[256,128]{1,0:T(8,128)S(1)} %get-tuple-element.83), channel_id=1, source_target_pairs={{0,2},{1,3},{2,0},{3,1},{4,6},{5,7},{6,4},{7,5},{8,10},{9,11},{10,... | collective-permute-start | bytes 393224 | tf_op jit(solution)/shard_map/ppermute | solution.py:277
  37.0 1.2 %collective-permute-start.9 = (f32[256,128]{1,0:T(8,128)S(1)}, f32[256,128]{1,0:T(8,128)S(1)}, u32[]{:S(2)}, u32[]{:S(2)}) collective-permute-start(f32[256,128]{1,0:T(8,128)S(1)} %get-tuple-element.84), channel_id=1, source_target_pairs={{0,3},{1,0},{2,1},{3,2},{4,7},{5,4},{6,5},{7,6},{8,11},{9,8},{10,9... | collective-permute-start | bytes 393224 | tf_op jit(solution)/shard_map/ppermute | solution.py:277
  38.2 1.8 %add_carry.2 = (bf16[1536,512]{1,0:T(8,128)(2,1)}, bf16[1536,512]{1,0:T(8,128)(2,1)}, bf16[1536,512]{1,0:T(8,128)(2,1)}, bf16[1536,512]{1,0:T(8,128)(2,1)}) custom-call(bf16[1536,512]{1,0:T(8,128)(2,1)S(1)} %get-tuple-element.40.q_ref.q.refs_0_, bf16[1536,512]{1,0:T(8,128)(2,1)S(1)} %get-tuple-element.41.k_ref.k.refs_1_, ...), custom_call_target="tpu_custom_call" | custom-call | flops 1500000000 | bytes 1024 | tf_op jit(solution)/shard_map/add_carry/pallas_call | solution.py:244
  40.0 1.2 %collective-permute-done.7.refs_10_ = f32[256,128]{1,0:T(8,128)S(1)} collective-permute-done((f32[256,128]{1,0:T(8,128)S(1)}, f32[256,128]{1,0:T(8,128)S(1)}, u32[]{:S(2)}, u32[]{:S(2)}) %collective-permute-start.7) | collective-permute-done | bytes 131104 | tf_op jit(solution)/shard_map/ppermute | solution.py:277
  41.2 1.6 %collective-permute-done.8.refs_11_ = f32[256,128]{1,0:T(8,128)S(1)} collective-permute-done((f32[256,128]{1,0:T(8,128)S(1)}, f32[256,128]{1,0:T(8,128)S(1)}, u32[]{:S(2)}, u32[]{:S(2)}) %collective-permute-start.8) | collective-permute-done | bytes 131104 | tf_op jit(solution)/shard_map/ppermute | solution.py:277
  42.8 0.0 collective-permute-done.9.refs_12_
  42.8 3.8 %add_carry.3 = (bf16[1536,512]{1,0:T(8,128)(2,1)}, bf16[1536,512]{1,0:T(8,128)(2,1)}, bf16[1536,512]{1,0:T(8,128)(2,1)}, bf16[1536,512]{1,0:T(8,128)(2,1)}) custom-call(bf16[1536,512]{1,0:T(8,128)(2,1)S(1)} %get-tuple-element.40.q_ref.q.refs_0_, ...), custom_call_target="tpu_custom_call", output_to_operand_aliasing={{0}: (13, {}), {1}: (14, {}), {2}: (15, {}), {3}: (16, {})} | custom-call | flops 4499999744 | bytes 1024 | tf_op jit(solution)/shard_map/add_carry/pallas_call | solution.py:244
  (5 shorter events, 0.1 us)
Async XLA Ops:
  4.1 10.4 %collective-permute-start = (f32[256,128]{1,0:T(8,128)S(1)}, f32[256,128]{1,0:T(8,128)S(1)}, u32[]{:S(2)}, u32[]{:S(2)}) collective-permute-start(f32[256,128]{1,0:T(8,128)S(1)} %get-tuple-element.63), channel_id=1, source_target_pairs={{0,1},{1,2},{2,3},{3,0},{4,5},{5,6},{6,7},{7,4},{8,9},{9,10},{10,1... | collective-permute-start | bytes 393224 | tf_op jit(solution)/shard_map/ppermute | solution.py:277
  5.7 9.5 %collective-permute-start.1 = (f32[256,128]{1,0:T(8,128)S(1)}, f32[256,128]{1,0:T(8,128)S(1)}, u32[]{:S(2)}, u32[]{:S(2)}) collective-permute-start(f32[256,128]{1,0:T(8,128)S(1)} %get-tuple-element.64), channel_id=1, source_target_pairs={{0,2},{1,3},{2,0},{3,1},{4,6},{5,7},{6,4},{7,5},{8,10},{9,11},{10,... | collective-permute-start | bytes 393224 | tf_op jit(solution)/shard_map/ppermute | solution.py:277
  8.6 6.6 %collective-permute-start.2 = (f32[256,128]{1,0:T(8,128)S(1)}, f32[256,128]{1,0:T(8,128)S(1)}, u32[]{:S(2)}, u32[]{:S(2)}) collective-permute-start(f32[256,128]{1,0:T(8,128)S(1)} %get-tuple-element.65), channel_id=1, source_target_pairs={{0,3},{1,0},{2,1},{3,2},{4,7},{5,4},{6,5},{7,6},{8,11},{9,8},{10,9... | collective-permute-start | bytes 393224 | tf_op jit(solution)/shard_map/ppermute | solution.py:277
  15.3 5.2 %collective-permute-start.3 = (f32[256,128]{1,0:T(8,128)S(1)}, f32[256,128]{1,0:T(8,128)S(1)}, u32[]{:S(2)}, u32[]{:S(2)}) collective-permute-start(f32[256,128]{1,0:T(8,128)S(1)} %add_add_fusion), channel_id=1, source_target_pairs={{0,4},{1,5},{2,6},{3,7},{4,0},{5,1},{6,2},{7,3},{8,12},{9,13},{10,... | collective-permute-start | bytes 393224 | tf_op jit(solution)/shard_map/ppermute | solution.py:268
  20.5 11.4 %collective-permute-start.5 = (f32[128,128]{1,0:T(8,128)S(1)}, f32[128,128]{1,0:T(8,128)S(1)}, u32[]{:S(2)}, u32[]{:S(2)}) collective-permute-start(f32[128,128]{1,0:T(8,128)S(1)} %get-tuple-element.86), channel_id=1, source_target_pairs={{0,20},{1,21},{2,22},{3,23},{4,16},{5,17},{6,18},{7,19},{8,28},{9,... | collective-permute-start | bytes 196616 | tf_op jit(solution)/shard_map/ppermute | solution.py:268
  26.5 7.5 %collective-permute-start.6 = (f32[128,128]{1,0:T(8,128)S(1)}, f32[128,128]{1,0:T(8,128)S(1)}, u32[]{:S(2)}, u32[]{:S(2)}) collective-permute-start(f32[128,128]{1,0:T(8,128)S(1)} %get-tuple-element.86), channel_id=1, source_target_pairs={{0,28},{1,29},{2,30},{3,31},{4,24},{5,25},{6,26},{7,27},{8,20},{9,... | collective-permute-start | bytes 196616 | tf_op jit(solution)/shard_map/ppermute | solution.py:268
  27.5 4.5 %collective-permute-start.4 = (f32[128,128]{1,0:T(8,128)S(1)}, f32[128,128]{1,0:T(8,128)S(1)}, u32[]{:S(2)}, u32[]{:S(2)}) collective-permute-start(f32[128,128]{1,0:T(8,128)S(1)} %get-tuple-element.78), channel_id=1, source_target_pairs={{0,12},{1,13},{2,14},{3,15},{4,8},{5,9},{6,10},{7,11},{8,4},{9,5},... | collective-permute-start | bytes 196616 | tf_op jit(solution)/shard_map/ppermute | solution.py:268
  34.1 7.2 %collective-permute-start.7 = (f32[256,128]{1,0:T(8,128)S(1)}, f32[256,128]{1,0:T(8,128)S(1)}, u32[]{:S(2)}, u32[]{:S(2)}) collective-permute-start(f32[256,128]{1,0:T(8,128)S(1)} %get-tuple-element.85), channel_id=1, source_target_pairs={{0,1},{1,2},{2,3},{3,0},{4,5},{5,6},{6,7},{7,4},{8,9},{9,10},{10,1... | collective-permute-start | bytes 393224 | tf_op jit(solution)/shard_map/ppermute | solution.py:277
  34.1 8.7 %collective-permute-start.8 = (f32[256,128]{1,0:T(8,128)S(1)}, f32[256,128]{1,0:T(8,128)S(1)}, u32[]{:S(2)}, u32[]{:S(2)}) collective-permute-start(f32[256,128]{1,0:T(8,128)S(1)} %get-tuple-element.83), channel_id=1, source_target_pairs={{0,2},{1,3},{2,0},{3,1},{4,6},{5,7},{6,4},{7,5},{8,10},{9,11},{10,... | collective-permute-start | bytes 393224 | tf_op jit(solution)/shard_map/ppermute | solution.py:277
  37.0 5.8 %collective-permute-start.9 = (f32[256,128]{1,0:T(8,128)S(1)}, f32[256,128]{1,0:T(8,128)S(1)}, u32[]{:S(2)}, u32[]{:S(2)}) collective-permute-start(f32[256,128]{1,0:T(8,128)S(1)} %get-tuple-element.84), channel_id=1, source_target_pairs={{0,3},{1,0},{2,1},{3,2},{4,7},{5,4},{6,5},{7,6},{8,11},{9,8},{10,9... | collective-permute-start | bytes 393224 | tf_op jit(solution)/shard_map/ppermute | solution.py:277

commit v4 on v2

--- a/solution.py
+++ b/solution.py
@@ -262,6 +262,15 @@
     def swap(x, zmap):
         return lax.ppermute(x, "seq", moves(zmap, lambda b: b))
 
+    def split_swap(x, even, odd):
+        ring = NY * NZ
+        pairs = [
+            (p * ring + i, p * ring + j)
+            for p in range(lax.axis_size("dp"))
+            for i, j in moves(lambda a: a ^ (odd if p & 1 else even), lambda b: b)
+        ]
+        return lax.ppermute(x, ("dp", "seq"), pairs)
+
     def turn(x, d):
         return lax.ppermute(x, "seq", moves(lambda a: a, lambda b: (b + d) % NY))
 
@@ -280,7 +289,7 @@
     total = total + pair
     four = swap(jnp.where(up, total[DH:], total[:DH]), lambda a: a ^ 3)
     across = jnp.where(high, total[DH:], total[:DH])
-    eight = swap(across, lambda a: a ^ 5), swap(across, lambda a: 7 - a)
+    eight = split_swap(across, 5, 7), split_swap(across, 7, 5)
     eight = eight[0] + eight[1]
     last = jnp.concatenate(
         [

time: 46 us -> 46.5 us (1.011)
    ppermute x0 -> x2, starting transfers between devices: none -> 6.93 us  [split_swap(): return lax.ppermute(x, ('dp', 'seq'), pairs)]
    ppermute x4 -> x2, starting transfers between devices: 7.24 us -> 0.39 us  [swap(): return lax.ppermute(x, 'seq', moves(zmap, lambda b: b))]
    ppermute x0 -> x2, waiting for transfers between devices: none -> 1.48 us  [split_swap(): return lax.ppermute(x, ('dp', 'seq'), pairs)]
    ppermute x4 -> x2, waiting for transfers between devices: 6.73 us -> 5.58 us  [swap(): return lax.ppermute(x, 'seq', moves(zmap, lambda b: b))]
where the time goes in v4:
time: 46.5 us; the launch traced here: 46.2 us
  starting transfers between devices  18.8 us (40%)
  Pallas kernels  17.8 us (38%)
  waiting for transfers between devices  8.58 us (18%)
  between operations  0.91 us (2%)
    ppermute x6, starting transfers between devices, turn(): return lax.ppermute(x, 'seq', moves(lambda a: a, lambda b: (b + d) % NY))  11.5 us
    pallas_call x4, Pallas kernels, local_products(): pl.pallas_call(functools.partial(local_kernel, scale, h, blocks), in_spec...  8.21 us
    ppermute x2, starting transfers between devices, split_swap(): return lax.ppermute(x, ('dp', 'seq'), pairs)  6.93 us
    ppermute x2, waiting for transfers between devices, swap(): return lax.ppermute(x, 'seq', moves(zmap, lambda b: b))  5.58 us
    pallas_call x2, Pallas kernels, add_carry(): pl.pallas_call(functools.partial(carry_kernel, scale, steps, blocks), in_...  5.54 us
    pallas_call x1, Pallas kernels, device_sums(): pl.pallas_call(sums_kernel, in_specs=[SM] * 3 + [HB] * 4, out_specs=[VM]...  3.45 us
    ppermute x6, waiting for transfers between devices, turn(): return lax.ppermute(x, 'seq', moves(lambda a: a, lambda b: (b + d) % NY))  1.52 us
    ppermute x2, waiting for transfers between devices, split_swap(): return lax.ppermute(x, ('dp', 'seq'), pairs)  1.48 us
  transfers between devices with their start and end apart: 10, of which 6 were waited for; matrix products, arithmetic and copies ran while one was open for 0% of the time, Pallas kernels for 23%

profile of v4, /device:TPU:38, one launch (start us, length us, event | category | flops | bytes accessed | tf_op | source)
XLA Modules:
  0.0 46.2 jit_solution(12227722973489846673)
XLA Ops:
  0.6 3.5 %device_sums.1 = (bf16[1536,512]{1,0:T(8,128)(2,1)S(1)}, bf16[1536,512]{1,0:T(8,128)(2,1)S(1)}, bf16[1536,512]{1,0:T(8,128)(2,1)S(1)}, bf16[1536,512]{1,0:T(8,12...) custom-call(s32[1]{0:T(128)} %bitcast.me_ref, ...), custom_call_target="tpu_custom_call" | custom-call | tf_op jit(solution)/shard_map/device_sums/pallas_call | solution.py:95
  4.1 1.7 %collective-permute-start = (f32[256,128]{1,0:T(8,128)S(1)}, f32[256,128]{1,0:T(8,128)S(1)}, u32[]{:S(2)}, u32[]{:S(2)}) collective-permute-start(f32[256,128]{1,0:T(8,128)S(1)} %get-tuple-element.61), channel_id=1, source_target_pairs={{0,1},{1,2},{2,3},{3,0},{4,5},{5,6},{6,7},{7,4},{8,9},{9,10},{10,1... | collective-permute-start | bytes 393224 | tf_op jit(solution)/shard_map/ppermute | solution.py:275
  5.8 2.9 %collective-permute-start.1 = (f32[256,128]{1,0:T(8,128)S(1)}, f32[256,128]{1,0:T(8,128)S(1)}, u32[]{:S(2)}, u32[]{:S(2)}) collective-permute-start(f32[256,128]{1,0:T(8,128)S(1)} %get-tuple-element.62), channel_id=1, source_target_pairs={{0,2},{1,3},{2,0},{3,1},{4,6},{5,7},{6,4},{7,5},{8,10},{9,11},{10,... | collective-permute-start | bytes 393224 | tf_op jit(solution)/shard_map/ppermute | solution.py:275
  8.7 1.3 %collective-permute-start.2 = (f32[256,128]{1,0:T(8,128)S(1)}, f32[256,128]{1,0:T(8,128)S(1)}, u32[]{:S(2)}, u32[]{:S(2)}) collective-permute-start(f32[256,128]{1,0:T(8,128)S(1)} %get-tuple-element.63), channel_id=1, source_target_pairs={{0,3},{1,0},{2,1},{3,2},{4,7},{5,4},{6,5},{7,6},{8,11},{9,8},{10,9... | collective-permute-start | bytes 393224 | tf_op jit(solution)/shard_map/ppermute | solution.py:275
  10.0 2.1 %local_products.4 = (f32[1536,512]{1,0:T(8,128)S(1)}, f32[1536,512]{1,0:T(8,128)S(1)}, f32[1536,512]{1,0:T(8,128)S(1)}, f32[1536,512]{1,0:T(8,128)S(1)}) custom-call(bf16[1536,512]{1,0:T(8,128)(2,1)S(1)} %get-tuple-element.38.q_ref.q.refs_0_, bf16[1536,512]{1,0:T(8,128)(2,1)S(1)} %get-tuple-element.39.k_ref.k.refs_1_, ...), custom_call_target="tpu_custom_call" | custom-call | flops 2000000000 | bytes 1024 | tf_op jit(solution)/shard_map/local_products/pallas_call | solution.py:160
  12.1 0.4 own_sums.1
  12.5 2.1 %local_products.5 = (f32[1536,512]{1,0:T(8,128)S(1)}, f32[1536,512]{1,0:T(8,128)S(1)}, f32[1536,512]{1,0:T(8,128)S(1)}, f32[1536,512]{1,0:T(8,128)S(1)}) custom-call(bf16[1536,512]{1,0:T(8,128)(2,1)S(1)} %get-tuple-element.38.q_ref.q.refs_0_, ...), custom_call_target="tpu_custom_call", output_to_operand_aliasing={{0}: (4, {}), {1}: (5, {}), {2}: (6, {}), {3}: (7, {})} | custom-call | flops 2000000000 | bytes 1024 | tf_op jit(solution)/shard_map/local_products/pallas_call | solution.py:160
  14.5 0.0 collective-permute-done.g1
  14.6 0.1 collective-permute-done.1.g2
  14.7 0.0 collective-permute-done.2.g3
  14.7 0.2 collective-permute-start.3
  14.9 2.0 %local_products.6 = (f32[1536,512]{1,0:T(8,128)S(1)}, f32[1536,512]{1,0:T(8,128)S(1)}, f32[1536,512]{1,0:T(8,128)S(1)}, f32[1536,512]{1,0:T(8,128)S(1)}) custom-call(bf16[1536,512]{1,0:T(8,128)(2,1)S(1)} %get-tuple-element.38.q_ref.q.refs_0_, ...), custom_call_target="tpu_custom_call", output_to_operand_aliasing={{0}: (4, {}), {1}: (5, {}), {2}: (6, {}), {3}: (7, {})} | custom-call | flops 2000000000 | bytes 1024 | tf_op jit(solution)/shard_map/local_products/pallas_call | solution.py:160
  17.0 2.8 %collective-permute-done.3.pair = f32[256,128]{1,0:T(8,128)S(1)} collective-permute-done((f32[256,128]{1,0:T(8,128)S(1)}, f32[256,128]{1,0:T(8,128)S(1)}, u32[]{:S(2)}, u32[]{:S(2)}) %collective-permute-start.3) | collective-permute-done | bytes 131104 | tf_op jit(solution)/shard_map/ppermute | solution.py:263
  19.8 6.1 %collective-permute-start.5 = (f32[128,128]{1,0:T(8,128)S(1)}, f32[128,128]{1,0:T(8,128)S(1)}, u32[]{:S(2)}, u32[]{:S(2)}) collective-permute-start(f32[128,128]{1,0:T(8,128)S(1)} %get-tuple-element.78), channel_id=1, source_target_pairs={{0,20},{1,21},{2,22},{3,23},{4,16},{5,17},{6,18},{7,19},{8,28},{9,... | collective-permute-start | bytes 196616 | tf_op jit(solution)/shard_map/ppermute | solution.py:272
  25.9 0.8 %collective-permute-start.6 = (f32[128,128]{1,0:T(8,128)S(1)}, f32[128,128]{1,0:T(8,128)S(1)}, u32[]{:S(2)}, u32[]{:S(2)}) collective-permute-start(f32[128,128]{1,0:T(8,128)S(1)} %get-tuple-element.78), channel_id=1, source_target_pairs={{0,28},{1,29},{2,30},{3,31},{4,24},{5,25},{6,26},{7,27},{8,20},{9,... | collective-permute-start | bytes 196616 | tf_op jit(solution)/shard_map/ppermute | solution.py:272
  26.7 0.2 collective-permute-start.4
  26.9 2.1 %local_products.7 = (f32[1536,512]{1,0:T(8,128)S(1)}, f32[1536,512]{1,0:T(8,128)S(1)}, f32[1536,512]{1,0:T(8,128)S(1)}, f32[1536,512]{1,0:T(8,128)S(1)}) custom-call(bf16[1536,512]{1,0:T(8,128)(2,1)S(1)} %get-tuple-element.38.q_ref.q.refs_0_, ...), custom_call_target="tpu_custom_call", output_to_operand_aliasing={{0}: (4, {}), {1}: (5, {}), {2}: (6, {}), {3}: (7, {})} | custom-call | flops 2000000000 | bytes 1024 | tf_op jit(solution)/shard_map/local_products/pallas_call | solution.py:160
  29.0 0.2 make_ready.1
  29.2 2.8 %collective-permute-done.4 = f32[128,128]{1,0:T(8,128)S(1)} collective-permute-done((f32[128,128]{1,0:T(8,128)S(1)}, f32[128,128]{1,0:T(8,128)S(1)}, u32[]{:S(2)}, u32[]{:S(2)}) %collective-permute-start.4) | collective-permute-done | bytes 65568 | tf_op jit(solution)/shard_map/ppermute | solution.py:263
  31.9 0.0 collective-permute-done.5
  31.9 1.5 %collective-permute-done.6 = f32[128,128]{1,0:T(8,128)S(1)} collective-permute-done((f32[128,128]{1,0:T(8,128)S(1)}, f32[128,128]{1,0:T(8,128)S(1)}, u32[]{:S(2)}, u32[]{:S(2)}) %collective-permute-start.6) | collective-permute-done | bytes 65568 | tf_op jit(solution)/shard_map/ppermute | solution.py:272
  33.5 1.3 %collective-permute-start.7 = (f32[256,128]{1,0:T(8,128)S(1)}, f32[256,128]{1,0:T(8,128)S(1)}, u32[]{:S(2)}, u32[]{:S(2)}) collective-permute-start(f32[256,128]{1,0:T(8,128)S(1)} %get-tuple-element.77), channel_id=1, source_target_pairs={{0,1},{1,2},{2,3},{3,0},{4,5},{5,6},{6,7},{7,4},{8,9},{9,10},{10,1... | collective-permute-start | bytes 393224 | tf_op jit(solution)/shard_map/ppermute | solution.py:275
  34.8 2.5 %collective-permute-start.8 = (f32[256,128]{1,0:T(8,128)S(1)}, f32[256,128]{1,0:T(8,128)S(1)}, u32[]{:S(2)}, u32[]{:S(2)}) collective-permute-start(f32[256,128]{1,0:T(8,128)S(1)} %get-tuple-element.75), channel_id=1, source_target_pairs={{0,2},{1,3},{2,0},{3,1},{4,6},{5,7},{6,4},{7,5},{8,10},{9,11},{10,... | collective-permute-start | bytes 393224 | tf_op jit(solution)/shard_map/ppermute | solution.py:275
  37.3 1.8 %collective-permute-start.9 = (f32[256,128]{1,0:T(8,128)S(1)}, f32[256,128]{1,0:T(8,128)S(1)}, u32[]{:S(2)}, u32[]{:S(2)}) collective-permute-start(f32[256,128]{1,0:T(8,128)S(1)} %get-tuple-element.76), channel_id=1, source_target_pairs={{0,3},{1,0},{2,1},{3,2},{4,7},{5,4},{6,5},{7,6},{8,11},{9,8},{10,9... | collective-permute-start | bytes 393224 | tf_op jit(solution)/shard_map/ppermute | solution.py:275
  39.1 1.8 %add_carry.2 = (bf16[1536,512]{1,0:T(8,128)(2,1)}, bf16[1536,512]{1,0:T(8,128)(2,1)}, bf16[1536,512]{1,0:T(8,128)(2,1)}, bf16[1536,512]{1,0:T(8,128)(2,1)}) custom-call(s32[1]{0:T(128)} %bitcast.me_ref, bf16[1536,512]{1,0:T(8,128)(2,1)S(1)} %get-tuple-element.38.q_ref.q.refs_0_, bf16[1536,512]{1,0:T(8,128)(2,1)S(1)} %get-tuple-element.39.k_ref.k.refs_1_, ...), custom_call_target="tpu_custom_call" | custom-call | flops 1500000000 | bytes 1024 | tf_op jit(solution)/shard_map/add_carry/pallas_call | solution.py:237
  40.9 0.0 collective-permute-done.7.refs_10_
  40.9 0.8 %collective-permute-done.8.refs_11_ = f32[256,128]{1,0:T(8,128)S(1)} collective-permute-done((f32[256,128]{1,0:T(8,128)S(1)}, f32[256,128]{1,0:T(8,128)S(1)}, u32[]{:S(2)}, u32[]{:S(2)}) %collective-permute-start.8) | collective-permute-done | bytes 131104 | tf_op jit(solution)/shard_map/ppermute | solution.py:275
  41.6 0.6 %collective-permute-done.9.refs_12_ = f32[256,128]{1,0:T(8,128)S(1)} collective-permute-done((f32[256,128]{1,0:T(8,128)S(1)}, f32[256,128]{1,0:T(8,128)S(1)}, u32[]{:S(2)}, u32[]{:S(2)}) %collective-permute-start.9) | collective-permute-done | bytes 131104 | tf_op jit(solution)/shard_map/ppermute | solution.py:275
  42.3 3.7 %add_carry.3 = (bf16[1536,512]{1,0:T(8,128)(2,1)}, bf16[1536,512]{1,0:T(8,128)(2,1)}, bf16[1536,512]{1,0:T(8,128)(2,1)}, bf16[1536,512]{1,0:T(8,128)(2,1)}) custom-call(s32[1]{0:T(128)} %bitcast.me_ref, bf16[1536,512]{1,0:T(8,128)(2,1)S(1)} %get-tuple-element.38.q_ref.q.refs_0_, ...), custom_call_target="tpu_custom_call", output_to_operand_aliasing={{0}: (14, {}), {1}: (15, {}), {2}: (16, {}), {3}: (17, {})} | custom-call | flops 4499999744 | bytes 1024 | tf_op jit(solution)/shard_map/add_carry/pallas_call | solution.py:237
  (5 shorter events, 0.1 us)
Async XLA Ops:
  4.1 10.5 %collective-permute-start = (f32[256,128]{1,0:T(8,128)S(1)}, f32[256,128]{1,0:T(8,128)S(1)}, u32[]{:S(2)}, u32[]{:S(2)}) collective-permute-start(f32[256,128]{1,0:T(8,128)S(1)} %get-tuple-element.61), channel_id=1, source_target_pairs={{0,1},{1,2},{2,3},{3,0},{4,5},{5,6},{6,7},{7,4},{8,9},{9,10},{10,1... | collective-permute-start | bytes 393224 | tf_op jit(solution)/shard_map/ppermute | solution.py:275
  5.8 8.9 %collective-permute-start.1 = (f32[256,128]{1,0:T(8,128)S(1)}, f32[256,128]{1,0:T(8,128)S(1)}, u32[]{:S(2)}, u32[]{:S(2)}) collective-permute-start(f32[256,128]{1,0:T(8,128)S(1)} %get-tuple-element.62), channel_id=1, source_target_pairs={{0,2},{1,3},{2,0},{3,1},{4,6},{5,7},{6,4},{7,5},{8,10},{9,11},{10,... | collective-permute-start | bytes 393224 | tf_op jit(solution)/shard_map/ppermute | solution.py:275
  8.7 6.0 %collective-permute-start.2 = (f32[256,128]{1,0:T(8,128)S(1)}, f32[256,128]{1,0:T(8,128)S(1)}, u32[]{:S(2)}, u32[]{:S(2)}) collective-permute-start(f32[256,128]{1,0:T(8,128)S(1)} %get-tuple-element.63), channel_id=1, source_target_pairs={{0,3},{1,0},{2,1},{3,2},{4,7},{5,4},{6,5},{7,6},{8,11},{9,8},{10,9... | collective-permute-start | bytes 393224 | tf_op jit(solution)/shard_map/ppermute | solution.py:275
  14.7 5.1 %collective-permute-start.3 = (f32[256,128]{1,0:T(8,128)S(1)}, f32[256,128]{1,0:T(8,128)S(1)}, u32[]{:S(2)}, u32[]{:S(2)}) collective-permute-start(f32[256,128]{1,0:T(8,128)S(1)} %add_add_fusion), channel_id=1, source_target_pairs={{0,4},{1,5},{2,6},{3,7},{4,0},{5,1},{6,2},{7,3},{8,12},{9,13},{10,... | collective-permute-start | bytes 393224 | tf_op jit(solution)/shard_map/ppermute | solution.py:263
  19.8 12.1 %collective-permute-start.5 = (f32[128,128]{1,0:T(8,128)S(1)}, f32[128,128]{1,0:T(8,128)S(1)}, u32[]{:S(2)}, u32[]{:S(2)}) collective-permute-start(f32[128,128]{1,0:T(8,128)S(1)} %get-tuple-element.78), channel_id=1, source_target_pairs={{0,20},{1,21},{2,22},{3,23},{4,16},{5,17},{6,18},{7,19},{8,28},{9,... | collective-permute-start | bytes 196616 | tf_op jit(solution)/shard_map/ppermute | solution.py:272
  25.9 7.5 %collective-permute-start.6 = (f32[128,128]{1,0:T(8,128)S(1)}, f32[128,128]{1,0:T(8,128)S(1)}, u32[]{:S(2)}, u32[]{:S(2)}) collective-permute-start(f32[128,128]{1,0:T(8,128)S(1)} %get-tuple-element.78), channel_id=1, source_target_pairs={{0,28},{1,29},{2,30},{3,31},{4,24},{5,25},{6,26},{7,27},{8,20},{9,... | collective-permute-start | bytes 196616 | tf_op jit(solution)/shard_map/ppermute | solution.py:272
  26.7 5.2 %collective-permute-start.4 = (f32[128,128]{1,0:T(8,128)S(1)}, f32[128,128]{1,0:T(8,128)S(1)}, u32[]{:S(2)}, u32[]{:S(2)}) collective-permute-start(f32[128,128]{1,0:T(8,128)S(1)} %get-tuple-element.79), channel_id=1, source_target_pairs={{0,12},{1,13},{2,14},{3,15},{4,8},{5,9},{6,10},{7,11},{8,4},{9,5},... | collective-permute-start | bytes 196616 | tf_op jit(solution)/shard_map/ppermute | solution.py:263
  33.5 7.4 %collective-permute-start.7 = (f32[256,128]{1,0:T(8,128)S(1)}, f32[256,128]{1,0:T(8,128)S(1)}, u32[]{:S(2)}, u32[]{:S(2)}) collective-permute-start(f32[256,128]{1,0:T(8,128)S(1)} %get-tuple-element.77), channel_id=1, source_target_pairs={{0,1},{1,2},{2,3},{3,0},{4,5},{5,6},{6,7},{7,4},{8,9},{9,10},{10,1... | collective-permute-start | bytes 393224 | tf_op jit(solution)/shard_map/ppermute | solution.py:275
  34.8 6.9 %collective-permute-start.8 = (f32[256,128]{1,0:T(8,128)S(1)}, f32[256,128]{1,0:T(8,128)S(1)}, u32[]{:S(2)}, u32[]{:S(2)}) collective-permute-start(f32[256,128]{1,0:T(8,128)S(1)} %get-tuple-element.75), channel_id=1, source_target_pairs={{0,2},{1,3},{2,0},{3,1},{4,6},{5,7},{6,4},{7,5},{8,10},{9,11},{10,... | collective-permute-start | bytes 393224 | tf_op jit(solution)/shard_map/ppermute | solution.py:275
  37.3 5.0 %collective-permute-start.9 = (f32[256,128]{1,0:T(8,128)S(1)}, f32[256,128]{1,0:T(8,128)S(1)}, u32[]{:S(2)}, u32[]{:S(2)}) collective-permute-start(f32[256,128]{1,0:T(8,128)S(1)} %get-tuple-element.76), channel_id=1, source_target_pairs={{0,3},{1,0},{2,1},{3,2},{4,7},{5,4},{6,5},{7,6},{8,11},{9,8},{10,9... | collective-permute-start | bytes 393224 | tf_op jit(solution)/shard_map/ppermute | solution.py:275

commit v5 on v2

--- a/solution.py
+++ b/solution.py
@@ -278,7 +278,7 @@
     total = got[0] + got[1] + got[2] + got[3]
     pair = swap(total, lambda a: a ^ 1)
     total = total + pair
-    four = swap(jnp.where(up, total[DH:], total[:DH]), lambda a: a ^ 3)
+    four = swap(jnp.where(up, total[DH:], total[:DH]), lambda a: a ^ 2)
     across = jnp.where(high, total[DH:], total[:DH])
     eight = swap(across, lambda a: a ^ 5), swap(across, lambda a: 7 - a)
     eight = eight[0] + eight[1]

time: 46 us -> 46 us (level)
  no operation moved by 1% of the time
where the time goes in v5:
time: 46 us; the launch traced here: 45.7 us
  starting transfers between devices  18.8 us (41%)
  Pallas kernels  17.8 us (39%)
  waiting for transfers between devices  8.07 us (18%)
  between operations  0.91 us (2%)
    ppermute x6, starting transfers between devices, turn(): return lax.ppermute(x, 'seq', moves(lambda a: a, lambda b: (b + d) % NY))  11.2 us
    pallas_call x4, Pallas kernels, local_products(): pl.pallas_call(functools.partial(local_kernel, scale, h, blocks), in_spec...  8.21 us
    ppermute x4, starting transfers between devices, swap(): return lax.ppermute(x, 'seq', moves(zmap, lambda b: b))  7.6 us
    ppermute x4, waiting for transfers between devices, swap(): return lax.ppermute(x, 'seq', moves(zmap, lambda b: b))  6.37 us
    pallas_call x2, Pallas kernels, add_carry(): pl.pallas_call(functools.partial(carry_kernel, scale, steps, blocks), in_...  5.54 us
    pallas_call x1, Pallas kernels, device_sums(): pl.pallas_call(sums_kernel, in_specs=[SM] * 3 + [HB] * 4, out_specs=[VM]...  3.45 us
    ppermute x6, waiting for transfers between devices, turn(): return lax.ppermute(x, 'seq', moves(lambda a: a, lambda b: (b + d) % NY))  1.7 us
  transfers between devices with their start and end apart: 10, of which 6 were waited for; matrix products, arithmetic and copies ran while one was open for 0% of the time, Pallas kernels for 23%

profile of v5, /device:TPU:38, one launch (start us, length us, event | category | flops | bytes accessed | tf_op | source)
XLA Modules:
  0.0 45.7 jit_solution(10834149853151634379)
XLA Ops:
  0.6 3.5 %device_sums.1 = (bf16[1536,512]{1,0:T(8,128)(2,1)S(1)}, bf16[1536,512]{1,0:T(8,128)(2,1)S(1)}, bf16[1536,512]{1,0:T(8,128)(2,1)S(1)}, bf16[1536,512]{1,0:T(8,12...) custom-call(s32[1]{0:T(128)} %bitcast.me_ref, ...), custom_call_target="tpu_custom_call" | custom-call | tf_op jit(solution)/shard_map/device_sums/pallas_call | solution.py:95
  4.1 1.7 %collective-permute-start = (f32[256,128]{1,0:T(8,128)S(1)}, f32[256,128]{1,0:T(8,128)S(1)}, u32[]{:S(2)}, u32[]{:S(2)}) collective-permute-start(f32[256,128]{1,0:T(8,128)S(1)} %get-tuple-element.61), channel_id=1, source_target_pairs={{0,1},{1,2},{2,3},{3,0},{4,5},{5,6},{6,7},{7,4},{8,9},{9,10},{10,1... | collective-permute-start | bytes 393224 | tf_op jit(solution)/shard_map/ppermute | solution.py:266
  5.8 2.9 %collective-permute-start.1 = (f32[256,128]{1,0:T(8,128)S(1)}, f32[256,128]{1,0:T(8,128)S(1)}, u32[]{:S(2)}, u32[]{:S(2)}) collective-permute-start(f32[256,128]{1,0:T(8,128)S(1)} %get-tuple-element.62), channel_id=1, source_target_pairs={{0,2},{1,3},{2,0},{3,1},{4,6},{5,7},{6,4},{7,5},{8,10},{9,11},{10,... | collective-permute-start | bytes 393224 | tf_op jit(solution)/shard_map/ppermute | solution.py:266
  8.7 1.3 %collective-permute-start.2 = (f32[256,128]{1,0:T(8,128)S(1)}, f32[256,128]{1,0:T(8,128)S(1)}, u32[]{:S(2)}, u32[]{:S(2)}) collective-permute-start(f32[256,128]{1,0:T(8,128)S(1)} %get-tuple-element.63), channel_id=1, source_target_pairs={{0,3},{1,0},{2,1},{3,2},{4,7},{5,4},{6,5},{7,6},{8,11},{9,8},{10,9... | collective-permute-start | bytes 393224 | tf_op jit(solution)/shard_map/ppermute | solution.py:266
  10.0 2.1 %local_products.4 = (f32[1536,512]{1,0:T(8,128)S(1)}, f32[1536,512]{1,0:T(8,128)S(1)}, f32[1536,512]{1,0:T(8,128)S(1)}, f32[1536,512]{1,0:T(8,128)S(1)}) custom-call(bf16[1536,512]{1,0:T(8,128)(2,1)S(1)} %get-tuple-element.38.q_ref.q.refs_0_, bf16[1536,512]{1,0:T(8,128)(2,1)S(1)} %get-tuple-element.39.k_ref.k.refs_1_, ...), custom_call_target="tpu_custom_call" | custom-call | flops 2000000000 | bytes 1024 | tf_op jit(solution)/shard_map/local_products/pallas_call | solution.py:160
  12.1 0.4 own_sums.1
  12.5 2.1 %local_products.5 = (f32[1536,512]{1,0:T(8,128)S(1)}, f32[1536,512]{1,0:T(8,128)S(1)}, f32[1536,512]{1,0:T(8,128)S(1)}, f32[1536,512]{1,0:T(8,128)S(1)}) custom-call(bf16[1536,512]{1,0:T(8,128)(2,1)S(1)} %get-tuple-element.38.q_ref.q.refs_0_, ...), custom_call_target="tpu_custom_call", output_to_operand_aliasing={{0}: (4, {}), {1}: (5, {}), {2}: (6, {}), {3}: (7, {})} | custom-call | flops 2000000000 | bytes 1024 | tf_op jit(solution)/shard_map/local_products/pallas_call | solution.py:160
  14.5 0.0 collective-permute-done.g1
  14.6 0.1 collective-permute-done.1.g2
  14.7 0.0 collective-permute-done.2.g3
  14.7 0.2 collective-permute-start.3
  14.9 2.0 %local_products.6 = (f32[1536,512]{1,0:T(8,128)S(1)}, f32[1536,512]{1,0:T(8,128)S(1)}, f32[1536,512]{1,0:T(8,128)S(1)}, f32[1536,512]{1,0:T(8,128)S(1)}) custom-call(bf16[1536,512]{1,0:T(8,128)(2,1)S(1)} %get-tuple-element.38.q_ref.q.refs_0_, ...), custom_call_target="tpu_custom_call", output_to_operand_aliasing={{0}: (4, {}), {1}: (5, {}), {2}: (6, {}), {3}: (7, {})} | custom-call | flops 2000000000 | bytes 1024 | tf_op jit(solution)/shard_map/local_products/pallas_call | solution.py:160
  17.0 2.8 %collective-permute-done.3.pair = f32[256,128]{1,0:T(8,128)S(1)} collective-permute-done((f32[256,128]{1,0:T(8,128)S(1)}, f32[256,128]{1,0:T(8,128)S(1)}, u32[]{:S(2)}, u32[]{:S(2)}) %collective-permute-start.3) | collective-permute-done | bytes 131104 | tf_op jit(solution)/shard_map/ppermute | solution.py:263
  19.8 5.9 %collective-permute-start.5 = (f32[128,128]{1,0:T(8,128)S(1)}, f32[128,128]{1,0:T(8,128)S(1)}, u32[]{:S(2)}, u32[]{:S(2)}) collective-permute-start(f32[128,128]{1,0:T(8,128)S(1)} %get-tuple-element.78), channel_id=1, source_target_pairs={{0,20},{1,21},{2,22},{3,23},{4,16},{5,17},{6,18},{7,19},{8,28},{9,... | collective-permute-start | bytes 196616 | tf_op jit(solution)/shard_map/ppermute | solution.py:263
  25.7 1.0 %collective-permute-start.6 = (f32[128,128]{1,0:T(8,128)S(1)}, f32[128,128]{1,0:T(8,128)S(1)}, u32[]{:S(2)}, u32[]{:S(2)}) collective-permute-start(f32[128,128]{1,0:T(8,128)S(1)} %get-tuple-element.78), channel_id=1, source_target_pairs={{0,28},{1,29},{2,30},{3,31},{4,24},{5,25},{6,26},{7,27},{8,20},{9,... | collective-permute-start | bytes 196616 | tf_op jit(solution)/shard_map/ppermute | solution.py:263
  26.7 0.5 %collective-permute-start.4 = (f32[128,128]{1,0:T(8,128)S(1)}, f32[128,128]{1,0:T(8,128)S(1)}, u32[]{:S(2)}, u32[]{:S(2)}) collective-permute-start(f32[128,128]{1,0:T(8,128)S(1)} %get-tuple-element.79), channel_id=1, source_target_pairs={{0,8},{1,9},{2,10},{3,11},{4,12},{5,13},{6,14},{7,15},{8,0},{9,1},... | collective-permute-start | bytes 196616 | tf_op jit(solution)/shard_map/ppermute | solution.py:263
  27.2 2.1 %local_products.7 = (f32[1536,512]{1,0:T(8,128)S(1)}, f32[1536,512]{1,0:T(8,128)S(1)}, f32[1536,512]{1,0:T(8,128)S(1)}, f32[1536,512]{1,0:T(8,128)S(1)}) custom-call(bf16[1536,512]{1,0:T(8,128)(2,1)S(1)} %get-tuple-element.38.q_ref.q.refs_0_, ...), custom_call_target="tpu_custom_call", output_to_operand_aliasing={{0}: (4, {}), {1}: (5, {}), {2}: (6, {}), {3}: (7, {})} | custom-call | flops 2000000000 | bytes 1024 | tf_op jit(solution)/shard_map/local_products/pallas_call | solution.py:160
  29.3 0.2 make_ready.1
  29.4 2.6 %collective-permute-done.4 = f32[128,128]{1,0:T(8,128)S(1)} collective-permute-done((f32[128,128]{1,0:T(8,128)S(1)}, f32[128,128]{1,0:T(8,128)S(1)}, u32[]{:S(2)}, u32[]{:S(2)}) %collective-permute-start.4) | collective-permute-done | bytes 65568 | tf_op jit(solution)/shard_map/ppermute | solution.py:263
  32.1 0.0 collective-permute-done.5
  32.1 0.9 %collective-permute-done.6 = f32[128,128]{1,0:T(8,128)S(1)} collective-permute-done((f32[128,128]{1,0:T(8,128)S(1)}, f32[128,128]{1,0:T(8,128)S(1)}, u32[]{:S(2)}, u32[]{:S(2)}) %collective-permute-start.6) | collective-permute-done | bytes 65568 | tf_op jit(solution)/shard_map/ppermute | solution.py:263
  33.1 1.3 %collective-permute-start.7 = (f32[256,128]{1,0:T(8,128)S(1)}, f32[256,128]{1,0:T(8,128)S(1)}, u32[]{:S(2)}, u32[]{:S(2)}) collective-permute-start(f32[256,128]{1,0:T(8,128)S(1)} %get-tuple-element.77), channel_id=1, source_target_pairs={{0,1},{1,2},{2,3},{3,0},{4,5},{5,6},{6,7},{7,4},{8,9},{9,10},{10,1... | collective-permute-start | bytes 393224 | tf_op jit(solution)/shard_map/ppermute | solution.py:266
  34.4 2.4 %collective-permute-start.8 = (f32[256,128]{1,0:T(8,128)S(1)}, f32[256,128]{1,0:T(8,128)S(1)}, u32[]{:S(2)}, u32[]{:S(2)}) collective-permute-start(f32[256,128]{1,0:T(8,128)S(1)} %get-tuple-element.75), channel_id=1, source_target_pairs={{0,2},{1,3},{2,0},{3,1},{4,6},{5,7},{6,4},{7,5},{8,10},{9,11},{10,... | collective-permute-start | bytes 393224 | tf_op jit(solution)/shard_map/ppermute | solution.py:266
  36.8 1.6 %collective-permute-start.9 = (f32[256,128]{1,0:T(8,128)S(1)}, f32[256,128]{1,0:T(8,128)S(1)}, u32[]{:S(2)}, u32[]{:S(2)}) collective-permute-start(f32[256,128]{1,0:T(8,128)S(1)} %get-tuple-element.76), channel_id=1, source_target_pairs={{0,3},{1,0},{2,1},{3,2},{4,7},{5,4},{6,5},{7,6},{8,11},{9,8},{10,9... | collective-permute-start | bytes 393224 | tf_op jit(solution)/shard_map/ppermute | solution.py:266
  38.4 1.8 %add_carry.2 = (bf16[1536,512]{1,0:T(8,128)(2,1)}, bf16[1536,512]{1,0:T(8,128)(2,1)}, bf16[1536,512]{1,0:T(8,128)(2,1)}, bf16[1536,512]{1,0:T(8,128)(2,1)}) custom-call(s32[1]{0:T(128)} %bitcast.me_ref, bf16[1536,512]{1,0:T(8,128)(2,1)S(1)} %get-tuple-element.38.q_ref.q.refs_0_, bf16[1536,512]{1,0:T(8,128)(2,1)S(1)} %get-tuple-element.39.k_ref.k.refs_1_, ...), custom_call_target="tpu_custom_call" | custom-call | flops 1500000000 | bytes 1024 | tf_op jit(solution)/shard_map/add_carry/pallas_call | solution.py:237
  40.2 0.0 collective-permute-done.7.refs_10_
  40.2 1.0 %collective-permute-done.8.refs_11_ = f32[256,128]{1,0:T(8,128)S(1)} collective-permute-done((f32[256,128]{1,0:T(8,128)S(1)}, f32[256,128]{1,0:T(8,128)S(1)}, u32[]{:S(2)}, u32[]{:S(2)}) %collective-permute-start.8) | collective-permute-done | bytes 131104 | tf_op jit(solution)/shard_map/ppermute | solution.py:266
  41.1 0.6 %collective-permute-done.9.refs_12_ = f32[256,128]{1,0:T(8,128)S(1)} collective-permute-done((f32[256,128]{1,0:T(8,128)S(1)}, f32[256,128]{1,0:T(8,128)S(1)}, u32[]{:S(2)}, u32[]{:S(2)}) %collective-permute-start.9) | collective-permute-done | bytes 131104 | tf_op jit(solution)/shard_map/ppermute | solution.py:266
  41.7 3.7 %add_carry.3 = (bf16[1536,512]{1,0:T(8,128)(2,1)}, bf16[1536,512]{1,0:T(8,128)(2,1)}, bf16[1536,512]{1,0:T(8,128)(2,1)}, bf16[1536,512]{1,0:T(8,128)(2,1)}) custom-call(s32[1]{0:T(128)} %bitcast.me_ref, bf16[1536,512]{1,0:T(8,128)(2,1)S(1)} %get-tuple-element.38.q_ref.q.refs_0_, ...), custom_call_target="tpu_custom_call", output_to_operand_aliasing={{0}: (14, {}), {1}: (15, {}), {2}: (16, {}), {3}: (17, {})} | custom-call | flops 4499999744 | bytes 1024 | tf_op jit(solution)/shard_map/add_carry/pallas_call | solution.py:237
  (5 shorter events, 0.1 us)
Async XLA Ops:
  4.1 10.5 %collective-permute-start = (f32[256,128]{1,0:T(8,128)S(1)}, f32[256,128]{1,0:T(8,128)S(1)}, u32[]{:S(2)}, u32[]{:S(2)}) collective-permute-start(f32[256,128]{1,0:T(8,128)S(1)} %get-tuple-element.61), channel_id=1, source_target_pairs={{0,1},{1,2},{2,3},{3,0},{4,5},{5,6},{6,7},{7,4},{8,9},{9,10},{10,1... | collective-permute-start | bytes 393224 | tf_op jit(solution)/shard_map/ppermute | solution.py:266
  5.8 8.9 %collective-permute-start.1 = (f32[256,128]{1,0:T(8,128)S(1)}, f32[256,128]{1,0:T(8,128)S(1)}, u32[]{:S(2)}, u32[]{:S(2)}) collective-permute-start(f32[256,128]{1,0:T(8,128)S(1)} %get-tuple-element.62), channel_id=1, source_target_pairs={{0,2},{1,3},{2,0},{3,1},{4,6},{5,7},{6,4},{7,5},{8,10},{9,11},{10,... | collective-permute-start | bytes 393224 | tf_op jit(solution)/shard_map/ppermute | solution.py:266
  8.7 6.0 %collective-permute-start.2 = (f32[256,128]{1,0:T(8,128)S(1)}, f32[256,128]{1,0:T(8,128)S(1)}, u32[]{:S(2)}, u32[]{:S(2)}) collective-permute-start(f32[256,128]{1,0:T(8,128)S(1)} %get-tuple-element.63), channel_id=1, source_target_pairs={{0,3},{1,0},{2,1},{3,2},{4,7},{5,4},{6,5},{7,6},{8,11},{9,8},{10,9... | collective-permute-start | bytes 393224 | tf_op jit(solution)/shard_map/ppermute | solution.py:266
  14.7 5.1 %collective-permute-start.3 = (f32[256,128]{1,0:T(8,128)S(1)}, f32[256,128]{1,0:T(8,128)S(1)}, u32[]{:S(2)}, u32[]{:S(2)}) collective-permute-start(f32[256,128]{1,0:T(8,128)S(1)} %add_add_fusion), channel_id=1, source_target_pairs={{0,4},{1,5},{2,6},{3,7},{4,0},{5,1},{6,2},{7,3},{8,12},{9,13},{10,... | collective-permute-start | bytes 393224 | tf_op jit(solution)/shard_map/ppermute | solution.py:263
  19.8 12.3 %collective-permute-start.5 = (f32[128,128]{1,0:T(8,128)S(1)}, f32[128,128]{1,0:T(8,128)S(1)}, u32[]{:S(2)}, u32[]{:S(2)}) collective-permute-start(f32[128,128]{1,0:T(8,128)S(1)} %get-tuple-element.78), channel_id=1, source_target_pairs={{0,20},{1,21},{2,22},{3,23},{4,16},{5,17},{6,18},{7,19},{8,28},{9,... | collective-permute-start | bytes 196616 | tf_op jit(solution)/shard_map/ppermute | solution.py:263
  25.7 7.3 %collective-permute-start.6 = (f32[128,128]{1,0:T(8,128)S(1)}, f32[128,128]{1,0:T(8,128)S(1)}, u32[]{:S(2)}, u32[]{:S(2)}) collective-permute-start(f32[128,128]{1,0:T(8,128)S(1)} %get-tuple-element.78), channel_id=1, source_target_pairs={{0,28},{1,29},{2,30},{3,31},{4,24},{5,25},{6,26},{7,27},{8,20},{9,... | collective-permute-start | bytes 196616 | tf_op jit(solution)/shard_map/ppermute | solution.py:263
  26.7 5.3 %collective-permute-start.4 = (f32[128,128]{1,0:T(8,128)S(1)}, f32[128,128]{1,0:T(8,128)S(1)}, u32[]{:S(2)}, u32[]{:S(2)}) collective-permute-start(f32[128,128]{1,0:T(8,128)S(1)} %get-tuple-element.79), channel_id=1, source_target_pairs={{0,8},{1,9},{2,10},{3,11},{4,12},{5,13},{6,14},{7,15},{8,0},{9,1},... | collective-permute-start | bytes 196616 | tf_op jit(solution)/shard_map/ppermute | solution.py:263
  33.1 7.1 %collective-permute-start.7 = (f32[256,128]{1,0:T(8,128)S(1)}, f32[256,128]{1,0:T(8,128)S(1)}, u32[]{:S(2)}, u32[]{:S(2)}) collective-permute-start(f32[256,128]{1,0:T(8,128)S(1)} %get-tuple-element.77), channel_id=1, source_target_pairs={{0,1},{1,2},{2,3},{3,0},{4,5},{5,6},{6,7},{7,4},{8,9},{9,10},{10,1... | collective-permute-start | bytes 393224 | tf_op jit(solution)/shard_map/ppermute | solution.py:266
  34.4 6.7 %collective-permute-start.8 = (f32[256,128]{1,0:T(8,128)S(1)}, f32[256,128]{1,0:T(8,128)S(1)}, u32[]{:S(2)}, u32[]{:S(2)}) collective-permute-start(f32[256,128]{1,0:T(8,128)S(1)} %get-tuple-element.75), channel_id=1, source_target_pairs={{0,2},{1,3},{2,0},{3,1},{4,6},{5,7},{6,4},{7,5},{8,10},{9,11},{10,... | collective-permute-start | bytes 393224 | tf_op jit(solution)/shard_map/ppermute | solution.py:266
  36.8 5.0 %collective-permute-start.9 = (f32[256,128]{1,0:T(8,128)S(1)}, f32[256,128]{1,0:T(8,128)S(1)}, u32[]{:S(2)}, u32[]{:S(2)}) collective-permute-start(f32[256,128]{1,0:T(8,128)S(1)} %get-tuple-element.76), channel_id=1, source_target_pairs={{0,3},{1,0},{2,1},{3,2},{4,7},{5,4},{6,5},{7,6},{8,11},{9,8},{10,9... | collective-permute-start | bytes 393224 | tf_op jit(solution)/shard_map/ppermute | solution.py:266
